TPU v7x, 32 devices: a whole 2x2x4 slice. The times are simulated.
32 devices in a mesh: gx: 8 (over z, y), gy: 4 (over x, core).
Axes of the slice: x: 2, y: 2, z: 4, core: 2. Of those that a mesh axis runs over, the one named last changes fastest.
Arguments:
- state: float32 [8, 256, 512], P(None, 'gx', 'gy'), may hold values from -6 to 6
- load_vector: bfloat16 [8, 256, 512], P(None, 'gx', 'gy'), may hold values from -6 to 6
- active: int32 [256, 512], P('gx', 'gy'), may hold values 0 or 1
- stiff_band: float32 [3, 5], replicated, may hold values from -0.6 to 1.2
- mass_band: float32 [3, 5], replicated, may hold values from 0.1 to 0.6
- eig_basis: float32 [3, 16, 16], replicated, may hold values from -1.5 to 1.5
- eig_values: float32 [3, 16], replicated, may hold values from 0.2 to 5
- cut_cols: int32 [8, 4, 2], P('gx', 'gy'), may hold values from -1 to 63, as said below
- cut_inverse: bfloat16 [8, 4, 2, 16, 256, 256], P('gx', 'gy'), may hold values from -0.375 to 0.375
Outputs:
- smoothed: float32 [8, 256, 512], P(None, 'gx', 'gy')
Inputs may be any that keep to these rules, and one draw needn't show every extreme that they name: `cut_cols`: on each device the entries that are not -1 name distinct local patch columns; a device holds 0 to 2 such entries and some device holds 2.
All inputs are finite; a program needn't handle non-finite values. No bound on the sum of `active` on one device may be relied on, other than what follows from the above.
Results may differ from a plain program's by a relative error of at most 0.0003.
Values sent between devices are 32-bit elements; how exact they have to be, the bound alone decides.
A program may use at most 64 MiB of HBM per device.

v0:
```python
import jax
import jax.numpy as jnp
from jax import lax
from jax.sharding import PartitionSpec as P

BAND = 4
PATCH = 16


damping = 0.5


def with_halo(x, sides, width):
    for axis, dim in sides:
        size, length = (lax.axis_size(axis), x.shape[dim])
        up = [(i, (i + 1) % size) for i in range(size - 1)]
        down = [(j, i) for i, j in up]
        last = lax.slice_in_dim(x, length - width, length, axis=dim)
        initial = lax.slice_in_dim(x, 0, width, axis=dim)
        before = lax.ppermute(last, axis, up)
        after = lax.ppermute(initial, axis, down)
        x = jnp.concatenate([before, x, after], axis=dim)
    return x


def band_valid(values, coeffs, along):
    length = values.shape[along] - 2 * BAND
    result = coeffs[0] * lax.slice_in_dim(values, BAND, BAND + length, axis=along)
    for offset in range(1, BAND + 1):
        upper = lax.slice_in_dim(values, BAND + offset, BAND + offset + length, axis=along)
        lower = lax.slice_in_dim(values, BAND - offset, BAND - offset + length, axis=along)
        result = result + coeffs[offset] * (upper + lower)
    return result


def apply_operator(field, stiff_band, mass_band):
    padded = jnp.pad(field, ((BAND, BAND), (0, 0), (0, 0)))
    mass_z = band_valid(padded, mass_band[0], 0)
    stiff_z = band_valid(padded, stiff_band[0], 0)
    mass_xz = band_valid(mass_z, mass_band[1], 1)
    stiff_xz = band_valid(mass_z, stiff_band[1], 1)
    mass_x_stiff_z = band_valid(stiff_z, mass_band[1], 1)
    return band_valid(stiff_xz + mass_x_stiff_z, mass_band[2], 2) + band_valid(
        mass_xz, stiff_band[2], 2
    )


def fold_blocks(values, along, half_patch):
    lower = lax.slice_in_dim(values, 0, half_patch, axis=along + 1)
    upper = lax.slice_in_dim(values, half_patch, 2 * half_patch, axis=along + 1)
    widths_low = [(0, 0)] * values.ndim
    widths_high = [(0, 0)] * values.ndim
    widths_low[along] = (0, 1)
    widths_high[along] = (1, 0)
    return jnp.pad(lower, widths_low) + jnp.pad(upper, widths_high)


def settle_edges(middle, from_below, from_above, along):
    length = middle.shape[along]
    width = from_below.shape[along]
    widths_low = [(0, 0)] * middle.ndim
    widths_high = [(0, 0)] * middle.ndim
    widths_low[along] = (0, length - width)
    widths_high[along] = (length - width, 0)
    return middle + jnp.pad(from_below, widths_low) + jnp.pad(from_above, widths_high)


def on_device(
    state, load_vector, active, stiff_band, mass_band, eig_basis, eig_values, cut_cols, cut_inverse
):
    highest = lax.Precision.HIGHEST
    half_patch = PATCH // 2
    quarter = PATCH // 4
    depth, rows_x, rows_y = state.shape
    blocks_z = depth // half_patch
    blocks_x = rows_x // half_patch
    blocks_y = rows_y // half_patch
    columns = blocks_x * blocks_y
    live_mask = active.astype(jnp.float32)
    load_f = load_vector.astype(jnp.float32)
    stacked = jnp.concatenate([state, load_f, live_mask[None]], axis=0)
    wide = with_halo(stacked, (("gx", 1), ("gy", 2)), BAND + quarter)
    applied = apply_operator(wide[:depth], stiff_band, mass_band)
    inner = wide[depth:, BAND:-BAND, BAND:-BAND]
    resid_ext = inner[depth][None] * (inner[:depth] - applied)
    padded = jnp.pad(resid_ext, ((quarter, quarter), (0, 0), (0, 0)))
    blocks = padded.reshape(
        blocks_z + 1, half_patch, blocks_x + 1, half_patch, blocks_y + 1, half_patch
    )
    blocks = jnp.concatenate([blocks[:-1], blocks[1:]], axis=1)
    blocks = jnp.concatenate([blocks[:, :, :-1], blocks[:, :, 1:]], axis=3)
    blocks = jnp.concatenate([blocks[:, :, :, :, :-1], blocks[:, :, :, :, 1:]], axis=5)
    patches = blocks.transpose(0, 1, 2, 4, 3, 5).reshape(blocks_z, PATCH, columns, PATCH * PATCH)
    basis_z, basis_x, basis_y = (eig_basis[0], eig_basis[1], eig_basis[2])
    denom = 1.0 / (
        eig_values[0][:, None, None] + eig_values[1][None, :, None] + eig_values[2][None, None, :]
    )
    zmodes = jnp.einsum("zk,cznq->cknq", basis_z, patches, precision=highest)
    paired = (basis_x[:, None, :, None] * basis_y[None, :, None, :]).reshape(
        PATCH * PATCH, PATCH * PATCH
    )
    modes = jnp.einsum("qp,cknq->cknp", paired, zmodes, precision=highest)
    modes = modes * denom.reshape(PATCH, PATCH * PATCH)[None, :, None, :]
    modes = jnp.einsum("qp,cknp->cknq", paired, modes, precision=highest)
    fast = jnp.einsum("zk,cknq->cznq", basis_z, modes, precision=highest)
    select = (
        cut_cols.reshape(-1)[:, None] == jnp.arange(columns, dtype=jnp.int32)[None, :]
    ).astype(jnp.float32)
    taken = jnp.einsum("cknq,mn->mckq", zmodes, select, precision=highest).astype(jnp.bfloat16)
    inverse = cut_inverse.reshape(-1, PATCH, PATCH * PATCH, PATCH * PATCH)
    dense = jnp.einsum("mkpq,mckq->mckp", inverse, taken, preferred_element_type=jnp.float32)
    cut_back = jnp.einsum("zk,mckp->mczp", basis_z, dense, precision=highest)
    keep = 1.0 - jnp.sum(select, axis=0)
    merged = fast * keep[None, None, :, None] + jnp.einsum(
        "mczp,mn->cznp", cut_back, select, precision=highest
    )
    merged = merged.reshape(blocks_z, PATCH, blocks_x, blocks_y, PATCH, PATCH).transpose(
        0, 1, 2, 4, 3, 5
    )
    merged = fold_blocks(merged, 4, half_patch)
    merged = fold_blocks(merged, 2, half_patch)
    merged = fold_blocks(merged, 0, half_patch)
    spread = merged.reshape(depth + half_patch, rows_x + half_patch, rows_y + half_patch)[
        quarter : quarter + depth
    ]
    bordered = with_halo(spread, (("gx", 1), ("gy", 2)), quarter)
    along_x = settle_edges(
        bordered[:, 2 * quarter : 2 * quarter + rows_x],
        bordered[:, :quarter],
        bordered[:, -quarter:],
        1,
    )
    total = settle_edges(
        along_x[:, :, 2 * quarter : 2 * quarter + rows_y],
        along_x[:, :, :quarter],
        along_x[:, :, -quarter:],
        2,
    )
    return state + damping * live_mask[None] * total


def solution(mesh):
    placed = (
        P(None, "gx", "gy"),
        P(None, "gx", "gy"),
        P("gx", "gy"),
        P(),
        P(),
        P(),
        P(),
        P("gx", "gy", None),
        P("gx", "gy", None, None, None, None),
    )
    return jax.shard_map(
        on_device, mesh=mesh, in_specs=placed, out_specs=P(None, "gx", "gy"), check_vma=False
    )
```

profile of v0, /device:TPU:13, one launch (start us, length us, event | category | flops | bytes accessed | tf_op | source)
XLA Modules:
  0.0 154.0 jit_solution(12051447028676634302)
XLA Ops:
  0.0 0.9 convert_element_type.38
  0.9 0.7 convert_bitcast_fusion
  1.6 0.8 pad_maximum_fusion.12
  2.4 3.1 %collective-permute-start = (f32[17,8,128]{2,1,0:T(8,128)S(1)}, f32[17,8,128]{2,1,0:T(8,128)S(1)}, u32[]{:S(2)}, u32[]{:S(2)}) collective-permute-start(f32[17,8,128]{2,1,0:T(8,128)S(1)} %get-tuple-element.23), channel_id=1, source_target_pairs={{0,4},{4,8},{8,12},{12,16},{16,20},{20,24},{24,28},{1,5},{5,9},{9,... | collective-permute-start | bytes 208904 | tf_op jit(solution)/shard_map/ppermute | solution.py:20
  5.6 2.1 %collective-permute-start.1 = (f32[17,8,128]{2,1,0:T(8,128)S(1)}, f32[17,8,128]{2,1,0:T(8,128)S(1)}, u32[]{:S(2)}, u32[]{:S(2)}) collective-permute-start(f32[17,8,128]{2,1,0:T(8,128)S(1)} %get-tuple-element.24), channel_id=1, source_target_pairs={{4,0},{8,4},{12,8},{16,12},{20,16},{24,20},{28,24},{5,1},{9,5},{13... | collective-permute-start | bytes 208904 | tf_op jit(solution)/shard_map/ppermute | solution.py:21
  7.7 0.8 slice_bitcast_fusion.2
  8.6 0.1 add.307
  8.7 0.1 add.308
  8.8 0.1 add.311
  8.9 0.7 slice_bitcast_fusion.1
  9.6 0.7 convert_reduce_fusion
  10.4 0.2 broadcast_multiply_fusion
  10.6 1.9 %fusion.78 = (f32[1,1]{1,0:T(1,128)}, f32[1,1]{1,0:T(1,128)}, f32[1,1]{1,0:T(1,128)}, f32[1,1]{1,0:T(1,128)}, f32[1,1]{1,0:T(1,128)}, /*index=5*/f32[1,1]{1,0:T(...) fusion(f32[3,5]{1,0:T(4,128)} %param.12), kind=kLoop, calls=%fused_computation.158 | loop fusion | bytes 120 | tf_op jit(solution)/shard_map/slice | solution.py:28
  12.6 1.0 pad_maximum_fusion.1
  13.5 1.0 fusion.75
  14.5 4.2 %collective-permute-start.2 = (f32[17,48,8]{2,1,0:T(8,128)}, f32[17,48,8]{2,1,0:T(8,128)S(1)}, u32[]{:S(2)}, u32[]{:S(2)}) collective-permute-start(f32[17,48,8]{2,1,0:T(8,128)} %get-tuple-element.15), channel_id=1, source_target_pairs={{0,1},{1,2},{2,3},{4,5},{5,6},{6,7},{8,9},{9,10},{10,11},{12,13},{... | collective-permute-start | bytes 78344 | tf_op jit(solution)/shard_map/ppermute | solution.py:20
  18.8 1.9 %collective-permute-start.3 = (f32[17,48,8]{2,1,0:T(8,128)}, f32[17,48,8]{2,1,0:T(8,128)}, u32[]{:S(2)}, u32[]{:S(2)}) collective-permute-start(f32[17,48,8]{2,1,0:T(8,128)} %get-tuple-element.16), channel_id=1, source_target_pairs={{1,0},{2,1},{3,2},{5,4},{6,5},{7,6},{9,8},{10,9},{11,10},{13,12},{... | collective-permute-start | bytes 78344 | tf_op jit(solution)/shard_map/ppermute | solution.py:21
  20.7 0.7 fusion.77
  21.4 0.9 reshape.193
  22.3 1.7 %collective-permute-done.2 = f32[17,48,8]{2,1,0:T(8,128)S(1)} collective-permute-done((f32[17,48,8]{2,1,0:T(8,128)}, f32[17,48,8]{2,1,0:T(8,128)S(1)}, u32[]{:S(2)}, u32[]{:S(2)}) %collective-permute-start.2) | collective-permute-done | bytes 26144 | tf_op jit(solution)/shard_map/ppermute | solution.py:20
  24.1 4.4 %collective-permute-done.3 = f32[17,48,8]{2,1,0:T(8,128)} collective-permute-done((f32[17,48,8]{2,1,0:T(8,128)}, f32[17,48,8]{2,1,0:T(8,128)}, u32[]{:S(2)}, u32[]{:S(2)}) %collective-permute-start.3) | collective-permute-done | bytes 26144 | tf_op jit(solution)/shard_map/ppermute | solution.py:21
  28.4 1.1 pad_maximum_fusion.2
  29.6 6.5 %multiply_add_fusion = (f32[8,48,144]{2,1,0:T(8,128)S(1)}, f32[8,48,144]{2,1,0:T(8,128)S(1)}) fusion(f32[8,48,144]{2,1,0:T(8,128)S(1)} %pad_maximum_fusion.2, f32[]{:T(128)} %bitcast.18, f32[]{:T(128)} %bitcast.17, f32[]{:T(128)} %bitcast.16, f32[]{:T(128)} %bitcast.15, f32[]{:T(128)} %bitcast.14, f32[]{:T(128)} %bitcast.8, f32[]{:T(128)} %bitcast.7, ...), kind=kLoop, calls=%fused_computation.55 | loop fusion | flops 1437696 | bytes 663592 | tf_op jit(solution)/shard_map/add | solution.py:32
  36.2 3.3 %multiply_add_fusion.2 = f32[8,40,144]{2,1,0:T(8,128)S(1)} fusion(f32[8,48,144]{2,1,0:T(8,128)S(1)} %get-tuple-element.20, f32[]{:T(128)} %bitcast.22, f32[]{:T(128)} %bitcast.21, f32[]{:T(128)} %bitcast.20, f32[]{:T(128)} %bitcast.19, f32[]{:T(128)} %bitcast.13), kind=kLoop, calls=%fused_computation.104 | loop fusion | flops 599040 | bytes 1843220 | tf_op jit(solution)/shard_map/add | solution.py:32
  39.5 6.8 %fusion.39 = f32[8,40,144]{2,1,0:T(8,128)S(1)} fusion(f32[8,48,144]{2,1,0:T(8,128)S(1)} %get-tuple-element.19, f32[8,48,144]{2,1,0:T(8,128)S(1)} %get-tuple-element.20, f32[]{:T(128)} %bitcast.22, f32[]{:T(128)} %bitcast.21, f32[]{:T(128)} %bitcast.20, f32[]{:T(128)} %bitcast.19, f32[]{:T(128)} %bitcast.13, f32[]{:T(128)} %bitcast.12, f32[]{:T(128)} %bitcast.11, ...), kind=kLoop, calls=%fused_computation.89 | loop fusion | flops 1244160 | bytes 3502120 | tf_op jit(solution)/shard_map/add | solution.py:43
  46.3 0.8 maximum_bitcast_fusion.1
  47.1 8.7 %fusion.22 = f32[8,40,136]{2,1,0:T(8,128)S(1)} fusion(f32[8,40,144]{2,1,0:T(8,128)S(1)} %multiply_add_fusion.2, f32[8,40,144]{2,1,0:T(8,128)S(1)} %fusion.39, f32[17,48,8]{2,1,0:T(8,128)} %collective-permute-done.3, f32[17,48,8]{2,1,0:T(8,128)S(1)} %collective-permute-done.2, f32[17,8,128]{2,1,0:T(8,128)S(1)} %copy-done.3, ...), kind=kLoop, calls=%fused_computation.62 | loop fusion | flops 1523200 | bytes 3799336 | tf_op jit(solution)/shard_map/mul | solution.py:85
  55.9 2.3 %slice.516 = f32[1,8,5,8,17,8]{5,4,3,2,1,0:T(8,128)} reshape(f32[8,40,136]{2,1,0:T(8,128)S(1)} %get-tuple-element.21) | data formatting | bytes 348160 | tf_op jit(solution)/shard_map/slice | solution.py:90
  58.2 3.5 %copy.25 = f32[1,8,5,8,17,8]{4,5,3,2,1,0:T(8,128)S(1)} copy(f32[1,8,5,8,17,8]{5,4,3,2,1,0:T(8,128)} %slice.516) | data formatting | bytes 348160 | tf_op jit(solution)/shard_map/slice | solution.py:90
  61.8 2.3 %slice.518 = f32[1,8,5,8,17,8]{5,4,3,2,1,0:T(8,128)} reshape(f32[8,40,136]{2,1,0:T(8,128)S(1)} %get-tuple-element.22) | data formatting | bytes 348160 | tf_op jit(solution)/shard_map/slice | solution.py:90
  64.1 3.5 %copy.26 = f32[1,8,5,8,17,8]{4,5,3,2,1,0:T(8,128)S(1)} copy(f32[1,8,5,8,17,8]{5,4,3,2,1,0:T(8,128)} %slice.518) | data formatting | bytes 348160 | tf_op jit(solution)/shard_map/slice | solution.py:90
  67.6 0.2 fusion.5
  67.8 0.4 fusion.1
  68.2 1.7 %fusion.73 = (f32[1,16,4,16,16,8]{4,5,3,2,1,0:T(8,128)S(1)}, f32[1,16,4,16,16,8]{4,5,3,2,1,0:T(8,128)S(1)}) fusion(f32[1,16,4,16,17,8]{4,5,3,2,1,0:T(8,128)S(1)} %fusion.1), kind=kLoop, calls=%fused_computation.153 | loop fusion | bytes 2097152 | tf_op jit(solution)/shard_map/slice | solution.py:92
  69.9 4.2 %maximum_bitcast_fusion = f32[1,16,4,16,16,16]{3,5,4,2,1,0:T(8,128)} fusion(f32[1,16,4,16,16,8]{4,5,3,2,1,0:T(8,128)S(1)} %get-tuple-element.12, f32[1,16,4,16,16,8]{4,5,3,2,1,0:T(8,128)S(1)} %get-tuple-element.11), kind=kLoop, calls=%fused_computation.2 | loop fusion | flops 262144 | bytes 2097152 | tf_op jit(solution)/shard_map/transpose | solution.py:93
  74.0 10.7 %copy.27 = f32[1,16,4,16,16,16]{5,4,1,3,2,0:T(8,128)} copy(f32[1,16,4,16,16,16]{3,5,4,2,1,0:T(8,128)} %maximum_bitcast_fusion) | data formatting | bytes 2097152 | tf_op jit(solution)/shard_map/transpose | solution.py:93
  84.8 6.3 %reshape.186 = f32[16,64,256]{2,0,1:T(8,128)S(1)} reshape(f32[1,16,4,16,16,16]{5,4,1,3,2,0:T(8,128)} %copy.27) | data formatting | bytes 2097152 | tf_op jit(solution)/shard_map/reshape.68
  91.1 1.0 convolution_bitcast_fusion.1
  92.1 1.1 fusion.9
  93.2 1.5 convolution_multiply_fusion
  94.7 1.5 fusion.10
  96.2 1.2 fusion.2
  97.4 0.2 convolution_bitcast_fusion.2
  97.6 0.7 fusion.60
  98.3 1.5 fusion.8
  99.9 4.7 %reshape.190 = f32[1,16,4,16,16,16]{5,4,1,3,2,0:T(8,128)} reshape(f32[1,16,64,256]{3,1,2,0:T(8,128)S(1)} %fusion.8) | data formatting | bytes 2097152 | tf_op jit(solution)/shard_map/reshape | solution.py:117
  104.6 8.2 %copy.60 = f32[1,16,4,16,16,16]{5,3,4,2,1,0:T(8,128)S(1)} copy(f32[1,16,4,16,16,16]{5,4,1,3,2,0:T(8,128)} %reshape.190) | data formatting | bytes 2097152 | tf_op jit(solution)/shard_map/reshape | solution.py:117
  112.8 5.2 %fusion.72 = (f32[1,16,4,16,16,8]{5,4,3,2,1,0:T(8,128)S(1)}, f32[1,16,4,16,16,8]{5,4,3,2,1,0:T(8,128)}) fusion(f32[1,16,4,16,16,16]{5,4,3,2,1,0:T(8,128)S(1)} %bitcast.119), kind=kLoop, calls=%fused_computation.152 | loop fusion | bytes 2097152 | tf_op jit(solution)/shard_map/slice | solution.py:49
  118.0 4.9 %fusion = (f32[1,16,4,8,17,8]{5,4,3,2,1,0:T(8,128)S(1)}, f32[1,16,4,8,17,8]{5,4,3,2,1,0:T(8,128)S(1)}) fusion(f32[1,16,4,16,16,8]{5,4,3,2,1,0:T(8,128)S(1)} %get-tuple-element.9, f32[1,16,4,16,16,8]{5,4,3,2,1,0:T(8,128)} %get-tuple-element.10), kind=kLoop, calls=%fused_computation.7 | loop fusion | flops 139264 | bytes 1605632 | tf_op jit(solution)/shard_map/add | solution.py:55
  122.9 1.2 fusion.4
  124.2 3.9 %pad_add_fusion = f32[2,8,5,8,17,8]{5,4,3,2,1,0:T(8,128)} fusion(f32[1,8,5,8,17,8]{5,4,3,2,1,0:T(8,128)S(1)} %get-tuple-element.8, f32[1,8,5,8,17,8]{5,4,3,2,1,0:T(8,128)S(1)} %get-tuple-element.7), kind=kLoop, calls=%fused_computation.4 | loop fusion | flops 87040 | bytes 696320 | tf_op jit(solution)/shard_map/add | solution.py:55
  128.0 4.7 %reshape.191 = f32[16,40,136]{2,1,0:T(8,128)S(1)} reshape(f32[2,8,5,8,17,8]{5,4,3,2,1,0:T(8,128)} %pad_add_fusion) | data formatting | bytes 696320 | tf_op jit(solution)/shard_map/reshape | solution.py:123
  132.8 4.0 %collective-permute-start.4 = (f32[8,4,136]{2,1,0:T(4,128)S(1)}, f32[8,4,136]{2,1,0:T(4,128)S(1)}, u32[]{:S(2)}, u32[]{:S(2)}) collective-permute-start(f32[8,4,136]{2,1,0:T(4,128)S(1)} %get-tuple-element.13), channel_id=1, source_target_pairs={{0,4},{4,8},{8,12},{12,16},{16,20},{20,24},{24,28},{1,5},{5,9},{9,... | collective-permute-start | bytes 52232 | tf_op jit(solution)/shard_map/ppermute | solution.py:20
  136.8 1.9 %collective-permute-start.5 = (f32[8,4,136]{2,1,0:T(4,128)S(1)}, f32[8,4,136]{2,1,0:T(4,128)S(1)}, u32[]{:S(2)}, u32[]{:S(2)}) collective-permute-start(f32[8,4,136]{2,1,0:T(4,128)S(1)} %get-tuple-element.14), channel_id=1, source_target_pairs={{4,0},{8,4},{12,8},{16,12},{20,16},{24,20},{28,24},{5,1},{9,5},{13... | collective-permute-start | bytes 52232 | tf_op jit(solution)/shard_map/ppermute | solution.py:21
  138.8 3.6 %collective-permute-done.5 = f32[8,4,136]{2,1,0:T(4,128)S(1)} collective-permute-done((f32[8,4,136]{2,1,0:T(4,128)S(1)}, f32[8,4,136]{2,1,0:T(4,128)S(1)}, u32[]{:S(2)}, u32[]{:S(2)}) %collective-permute-start.5) | collective-permute-done | bytes 17440 | tf_op jit(solution)/shard_map/ppermute | solution.py:21
  142.4 0.1 fusion.76
  142.5 3.2 %collective-permute-start.6 = (f32[8,48,4]{2,1,0:T(8,128)S(1)}, f32[8,48,4]{2,1,0:T(8,128)S(1)}, u32[]{:S(2)}, u32[]{:S(2)}) collective-permute-start(f32[8,48,4]{2,1,0:T(8,128)S(1)} %get-tuple-element.17), channel_id=1, source_target_pairs={{0,1},{1,2},{2,3},{4,5},{5,6},{6,7},{8,9},{9,10},{10,11},{12,13},{... | collective-permute-start | bytes 18440 | tf_op jit(solution)/shard_map/ppermute | solution.py:20
  145.7 1.9 %collective-permute-start.7 = (f32[8,48,4]{2,1,0:T(8,128)S(1)}, f32[8,48,4]{2,1,0:T(8,128)S(1)}, u32[]{:S(2)}, u32[]{:S(2)}) collective-permute-start(f32[8,48,4]{2,1,0:T(8,128)S(1)} %get-tuple-element.18), channel_id=1, source_target_pairs={{1,0},{2,1},{3,2},{5,4},{6,5},{7,6},{9,8},{10,9},{11,10},{13,12},{... | collective-permute-start | bytes 18440 | tf_op jit(solution)/shard_map/ppermute | solution.py:21
  147.7 0.6 collective-permute-done.6
  148.3 4.4 %collective-permute-done.7 = f32[8,48,4]{2,1,0:T(8,128)S(1)} collective-permute-done((f32[8,48,4]{2,1,0:T(8,128)S(1)}, f32[8,48,4]{2,1,0:T(8,128)S(1)}, u32[]{:S(2)}, u32[]{:S(2)}) %collective-permute-start.7) | collective-permute-done | bytes 6176 | tf_op jit(solution)/shard_map/ppermute | solution.py:21
  152.7 0.3 pad_maximum_fusion.9
  153.0 0.1 fusion.46
  153.1 0.1 slice.603
  153.2 0.8 fusion.56
  (32 shorter events, 0.3 us)
Async XLA Ops:
  0.0 28.4 %copy-start = (f32[8,32,128]{2,1,0:T(8,128)S(1)}, f32[8,32,128]{2,1,0:T(8,128)}, u32[]{:S(2)}) copy-start(f32[8,32,128]{2,1,0:T(8,128)} %param.9) | copy-start | bytes 393220
  0.0 20.7 %copy-start.6 = (f32[3,5]{1,0:T(4,128)S(1)}, f32[3,5]{1,0:T(4,128)}, u32[]{:S(2)}) copy-start(f32[3,5]{1,0:T(4,128)} %param.13) | copy-start | bytes 184
  2.4 10.1 %collective-permute-start = (f32[17,8,128]{2,1,0:T(8,128)S(1)}, f32[17,8,128]{2,1,0:T(8,128)S(1)}, u32[]{:S(2)}, u32[]{:S(2)}) collective-permute-start(f32[17,8,128]{2,1,0:T(8,128)S(1)} %get-tuple-element.23), channel_id=1, source_target_pairs={{0,4},{4,8},{8,12},{12,16},{16,20},{20,24},{24,28},{1,5},{5,9},{9,... | collective-permute-start | bytes 208904 | tf_op jit(solution)/shard_map/ppermute | solution.py:20
  5.6 7.0 %collective-permute-start.1 = (f32[17,8,128]{2,1,0:T(8,128)S(1)}, f32[17,8,128]{2,1,0:T(8,128)S(1)}, u32[]{:S(2)}, u32[]{:S(2)}) collective-permute-start(f32[17,8,128]{2,1,0:T(8,128)S(1)} %get-tuple-element.24), channel_id=1, source_target_pairs={{4,0},{8,4},{12,8},{16,12},{20,16},{24,20},{28,24},{5,1},{9,5},{13... | collective-permute-start | bytes 208904 | tf_op jit(solution)/shard_map/ppermute | solution.py:21
  12.6 11.5 %copy-start.2 = (f32[17,8,128]{2,1,0:T(8,128)}, f32[17,8,128]{2,1,0:T(8,128)S(1)}, u32[]{:S(2)}) copy-start(f32[17,8,128]{2,1,0:T(8,128)S(1)} %collective-permute-done.1) | copy-start | bytes 208900
  14.5 9.5 %collective-permute-start.2 = (f32[17,48,8]{2,1,0:T(8,128)}, f32[17,48,8]{2,1,0:T(8,128)S(1)}, u32[]{:S(2)}, u32[]{:S(2)}) collective-permute-start(f32[17,48,8]{2,1,0:T(8,128)} %get-tuple-element.15), channel_id=1, source_target_pairs={{0,1},{1,2},{2,3},{4,5},{5,6},{6,7},{8,9},{9,10},{10,11},{12,13},{... | collective-permute-start | bytes 78344 | tf_op jit(solution)/shard_map/ppermute | solution.py:20
  18.8 9.7 %collective-permute-start.3 = (f32[17,48,8]{2,1,0:T(8,128)}, f32[17,48,8]{2,1,0:T(8,128)}, u32[]{:S(2)}, u32[]{:S(2)}) collective-permute-start(f32[17,48,8]{2,1,0:T(8,128)} %get-tuple-element.16), channel_id=1, source_target_pairs={{1,0},{2,1},{3,2},{5,4},{6,5},{7,6},{9,8},{10,9},{11,10},{13,12},{... | collective-permute-start | bytes 78344 | tf_op jit(solution)/shard_map/ppermute | solution.py:21
  36.1 10.1 %copy-start.3 = (f32[17,8,128]{2,1,0:T(8,128)S(1)}, f32[17,8,128]{2,1,0:T(8,128)}, u32[]{:S(2)}) copy-start(f32[17,8,128]{2,1,0:T(8,128)} %copy-done.2) | copy-start | bytes 208900
  84.8 6.3 %copy-start.4 = (f32[3,16,16]{2,1,0:T(8,128)S(1)}, f32[3,16,16]{2,1,0:T(8,128)}, u32[]{:S(2)}) copy-start(f32[3,16,16]{2,1,0:T(8,128)} %param.14) | copy-start | bytes 9220
  84.8 7.4 %copy-start.7 = (s32[1,1,2]{2,1,0:T(1,128)S(1)}, s32[1,1,2]{2,1,0:T(1,128)}, u32[]{:S(2)}) copy-start(s32[1,1,2]{2,1,0:T(1,128)} %param.16) | copy-start | bytes 28
  91.1 5.1 %copy-start.1 = (bf16[1,1,2,16,256,256]{5,4,3,2,1,0:T(8,128)(2,1)S(1)}, bf16[1,1,2,16,256,256]{5,4,3,2,1,0:T(8,128)(2,1)}, u32[]{:S(2)}) copy-start(bf16[1,1,2,16,256,256]{5,4,3,2,1,0:T(8,128)(2,1)} %param.17) | copy-start | bytes 12582916
  128.0 19.6 %copy-start.5 = (s32[32,128]{1,0:T(8,128)S(1)}, s32[32,128]{1,0:T(8,128)}, u32[]{:S(2)}) copy-start(s32[32,128]{1,0:T(8,128)} %param.11) | copy-start | bytes 49156
  128.0 25.0 %copy-start.8 = (pred[32]{0:T(512)(128)(4,1)S(1)}, pred[32]{0:T(512)(128)(4,1)}, u32[]{:S(2)}) copy-start(pred[32]{0:T(512)(128)(4,1)} %constant.11.clone.1) | copy-start | bytes 100
  132.7 20.5 %copy-start.9 = (pred[128]{0:T(512)(128)(4,1)S(1)}, pred[128]{0:T(512)(128)(4,1)}, u32[]{:S(2)}) copy-start(pred[128]{0:T(512)(128)(4,1)} %constant.12.clone.1) | copy-start | bytes 388
  132.8 6.0 %collective-permute-start.4 = (f32[8,4,136]{2,1,0:T(4,128)S(1)}, f32[8,4,136]{2,1,0:T(4,128)S(1)}, u32[]{:S(2)}, u32[]{:S(2)}) collective-permute-start(f32[8,4,136]{2,1,0:T(4,128)S(1)} %get-tuple-element.13), channel_id=1, source_target_pairs={{0,4},{4,8},{8,12},{12,16},{16,20},{20,24},{24,28},{1,5},{5,9},{9,... | collective-permute-start | bytes 52232 | tf_op jit(solution)/shard_map/ppermute | solution.py:20
  136.8 5.6 %collective-permute-start.5 = (f32[8,4,136]{2,1,0:T(4,128)S(1)}, f32[8,4,136]{2,1,0:T(4,128)S(1)}, u32[]{:S(2)}, u32[]{:S(2)}) collective-permute-start(f32[8,4,136]{2,1,0:T(4,128)S(1)} %get-tuple-element.14), channel_id=1, source_target_pairs={{4,0},{8,4},{12,8},{16,12},{20,16},{24,20},{28,24},{5,1},{9,5},{13... | collective-permute-start | bytes 52232 | tf_op jit(solution)/shard_map/ppermute | solution.py:21
  142.5 5.8 %collective-permute-start.6 = (f32[8,48,4]{2,1,0:T(8,128)S(1)}, f32[8,48,4]{2,1,0:T(8,128)S(1)}, u32[]{:S(2)}, u32[]{:S(2)}) collective-permute-start(f32[8,48,4]{2,1,0:T(8,128)S(1)} %get-tuple-element.17), channel_id=1, source_target_pairs={{0,1},{1,2},{2,3},{4,5},{5,6},{6,7},{8,9},{9,10},{10,11},{12,13},{... | collective-permute-start | bytes 18440 | tf_op jit(solution)/shard_map/ppermute | solution.py:20
  145.7 7.0 %collective-permute-start.7 = (f32[8,48,4]{2,1,0:T(8,128)S(1)}, f32[8,48,4]{2,1,0:T(8,128)S(1)}, u32[]{:S(2)}, u32[]{:S(2)}) collective-permute-start(f32[8,48,4]{2,1,0:T(8,128)S(1)} %get-tuple-element.18), channel_id=1, source_target_pairs={{1,0},{2,1},{3,2},{5,4},{6,5},{7,6},{9,8},{10,9},{11,10},{13,12},{... | collective-permute-start | bytes 18440 | tf_op jit(solution)/shard_map/ppermute | solution.py:21
where the time goes:
time: 155 us; the launch traced here: 154 us
  local copies, waits for them, and re-layouts  60 us (39%)
  other arithmetic  47.7 us (31%)
  starting transfers between devices  22.5 us (15%)
  waiting for transfers between devices  14.7 us (9%)
  matrix products  8.68 us (6%)
    ppermute x4, starting transfers between devices, with_halo(): before = lax.ppermute(last, axis, up)  14.6 us
    reshape x2, local copies, waits for them, and re-layouts, on_device(): merged.reshape(blocks_z, PATCH, blocks_x, blocks_y, PATCH, PATCH)  12.9 us
    ppermute x4, waiting for transfers between devices, with_halo(): after = lax.ppermute(initial, axis, down)  12.4 us
    slice x5, local copies, waits for them, and re-layouts, on_device(): blocks = jnp.concatenate([blocks[:-1], blocks[1:]], axis=1)  11.7 us
    transpose x1, local copies, waits for them, and re-layouts, on_device(): blocks.transpose(0, 1, 2, 4, 3, 5)  10.7 us
    add x3, other arithmetic, fold_blocks(): return jnp.pad(lower, widths_low) + jnp.pad(upper, widths_high)  10 us
    add x2, other arithmetic, band_valid(): result = result + coeffs[offset] * (upper + lower)  9.86 us
    mul x2, other arithmetic, on_device(): resid_ext = inner[depth][None] * (inner[:depth] - applied)  9.55 us
  transfers between devices with their start and end apart: 8, of which 5 were waited for; matrix products, arithmetic and copies ran while one was open for 4% of the time, Pallas kernels for 0%

commit v1 on v0

v1 whole, which is shorter than its diff:
```python
import functools

import jax
import jax.numpy as jnp
from jax import lax
from jax.experimental import pallas as pl
from jax.experimental.pallas import tpu as pltpu
from jax.sharding import PartitionSpec as P

BAND = 4
PATCH = 16
HALF = PATCH // 2
QUARTER = PATCH // 4
HALO = BAND + QUARTER
LANES = 128
MESH = pl.DeviceIdType.MESH
DIRS = [(dx, dy) for dx in (-1, 0, 1) for dy in (-1, 0, 1) if (dx, dy) != (0, 0)]

damping = 0.5
f32 = jnp.float32
bf16 = jnp.bfloat16


def iota(shape, dim):
    return lax.broadcasted_iota(jnp.int32, shape, dim)


def split(v):
    hi = v.astype(bf16)
    return hi, (v - hi.astype(f32)).astype(bf16)


def dot(a, b):
    return jnp.dot(a, b, preferred_element_type=f32)


def dot_nt(a, b):
    return lax.dot_general(a, b, (((1,), (1,)), ((), ())), preferred_element_type=f32)


def band_of(distance, taps):
    out = jnp.zeros(distance.shape, f32)
    for k in range(BAND + 1):
        out = jnp.where(distance == k, taps[k], out)
    return out


def inner_y(c, ry):
    u = (c - ry) % HALF
    halo = jnp.where(u < QUARTER, u - QUARTER, ry + u - QUARTER)
    return jnp.where(c < ry, c, jnp.where(c < ry + LANES // 2, -1000, halo))


def outer_y(r, ry):
    u = (r - ry) % HALF
    return jnp.where(r < ry, r, jnp.where(r < ry + LANES // 2, u - HALO, ry + u))


def kernel(
    sizes,
    state, load, active, stiff, mass, basis_s, basis, values, cols, inverse,
    out,
    ext, from_left, from_right, pack_left, pack_right,
    inv, yb_hi, yb_lo, wy_hi, wy_lo, sel, dinv,
    s_hi, s_lo, yv, xpq, r_hi, r_lo, uv, vv, tb_hi, tb_lo, tot, edge,
    up, down, left2, right2, corners,
    inv_sem, send1, recv1, send2, recv2,
):
    n_x, n_y = sizes
    nz, rx, ry = state.shape
    wide = rx + 2 * HALO
    slots = inverse.shape[0]
    blocks_x, blocks_y = rx // HALF, ry // HALF
    qx, qy = blocks_x * PATCH, blocks_y * PATCH
    full = ry + LANES
    me_x, me_y = lax.axis_index("gx"), lax.axis_index("gy")

    def exists(dx, dy):
        ok = None
        for d, me, n in ((dx, me_x, n_x), (dy, me_y, n_y)):
            if d:
                part = (me + d >= 0) & (me + d < n)
                ok = part if ok is None else ok & part
        return ok

    def device(dx, dy):
        return (jnp.clip(me_x + dx, 0, n_x - 1), jnp.clip(me_y + dy, 0, n_y - 1))

    fetch = pltpu.make_async_copy(inverse, inv, inv_sem)
    fetch.start()

    own = pl.ds(HALO, rx)
    for z in range(nz):
        ext[z, own, :] = state[z]
        ext[nz + z, own, :] = load[z].astype(f32)
    ext[2 * nz, own, :] = active[...].astype(f32)
    zeros = jnp.zeros((2 * nz + 1, HALO, ry), f32)
    ext[:, pl.ds(0, HALO), :] = zeros
    ext[:, pl.ds(HALO + rx, HALO), :] = zeros
    for ref in (from_left, from_right, up, down, left2, right2, corners):
        ref[...] = jnp.zeros(ref.shape, f32)

    barrier = pltpu.get_barrier_semaphore()
    count = jnp.int32(0)
    for d in DIRS:
        ok = exists(*d)
        count = count + ok.astype(jnp.int32)

        @pl.when(ok)
        def _(d=d):
            pl.semaphore_signal(barrier, inc=1, device_id=device(*d), device_id_type=MESH)

    lane = iota((rx, LANES), 1)
    to_right = jnp.zeros((rx, LANES), f32)
    to_left = jnp.zeros((rx, LANES), f32)
    act = ext[2 * nz, own, :]
    half = LANES // 2
    for z in range(nz):
        s = ext[z, own, :]
        l = pltpu.roll(ext[nz + z, own, :], (half + QUARTER + HALF * z) % LANES, 1)
        group = lane // HALF == z
        first = (lane // HALF == half // HALF + z) & (lane % HALF < QUARTER)
        second = (lane // HALF == half // HALF + z) & (lane % HALF >= QUARTER)
        to_right = jnp.where(group, pltpu.roll(s, (HALF + HALF * z) % LANES, 1), to_right)
        to_right = jnp.where(first, l, to_right)
        to_right = jnp.where(second, pltpu.roll(act, (half + HALF + HALF * z) % LANES, 1), to_right)
        to_left = jnp.where(group, pltpu.roll(s, HALF * z, 1) if z else s, to_left)
        to_left = jnp.where(second, l, to_left)
        to_left = jnp.where(first, pltpu.roll(act, (half + HALF * z) % LANES, 1), to_left)
    pack_right[...] = to_right
    pack_left[...] = to_left

    def copy1(i):
        dx, dy = DIRS[i]
        if dy == 0:
            src = ext.at[:, pl.ds(rx if dx > 0 else HALO, HALO), :]
            dst = ext.at[:, pl.ds(0 if dx > 0 else HALO + rx, HALO), :]
        else:
            pack = pack_right if dy > 0 else pack_left
            land = from_left if dy > 0 else from_right
            if dx == 0:
                src, dst = pack, land.at[pl.ds(HALO, rx), :]
            else:
                src = pack.at[pl.ds(rx - HALO if dx > 0 else 0, HALO), :]
                dst = land.at[pl.ds(0 if dx > 0 else HALO + rx, HALO), :]
        return pltpu.make_async_remote_copy(
            src_ref=src, dst_ref=dst, send_sem=send1.at[i], recv_sem=recv1.at[i],
            device_id=device(dx, dy), device_id_type=MESH,
        )

    def copy2(i):
        dx, dy = DIRS[i]
        if dy == 0:
            src = tot.at[:, pl.ds(HALO + rx if dx > 0 else 0, HALO), :]
            dst = up if dx > 0 else down
        elif dx == 0:
            src = edge.at[pl.ds(HALO, rx), :]
            dst = left2 if dy > 0 else right2
        else:
            src = edge.at[pl.ds(HALO + rx if dx > 0 else 0, HALO), :]
            dst = corners.at[(dx < 0) * 2 + (dy < 0)]
        return pltpu.make_async_remote_copy(
            src_ref=src, dst_ref=dst, send_sem=send2.at[i], recv_sem=recv2.at[i],
            device_id=device(dx, dy), device_id_type=MESH,
        )

    def start_all(copy):
        for i, d in enumerate(DIRS):
            @pl.when(exists(*d))
            def _(i=i):
                copy(i).start()

    def wait_recv_all(copy):
        for i, (dx, dy) in enumerate(DIRS):
            @pl.when(exists(-dx, -dy))
            def _(i=i):
                copy(i).wait_recv()

    def wait_send_all(copy):
        for i, d in enumerate(DIRS):
            @pl.when(exists(*d))
            def _(i=i):
                copy(i).wait_send()

    pl.semaphore_wait(barrier, count)
    start_all(copy1)

    distance = jnp.abs(outer_y(iota((full, full), 0), ry) - inner_y(iota((full, full), 1), ry))
    for j, taps in enumerate((mass, stiff)):
        h, l = split(band_of(distance, [taps[2, k] for k in range(BAND + 1)]))
        yb_hi[:, pl.ds(j * full, full)] = h
        yb_lo[:, pl.ds(j * full, full)] = l

    highest = lax.Precision.HIGHEST
    tile_y = jnp.dot(
        basis[2], (iota((PATCH, qy), 0) == iota((PATCH, qy), 1) % PATCH).astype(f32),
        precision=highest, preferred_element_type=f32,
    )
    place = inner_y(iota((full, qy), 0), ry) + QUARTER - HALF * (iota((full, qy), 1) // PATCH)
    wy = jnp.zeros((full, qy), f32)
    for t in range(PATCH):
        wy = jnp.where(place == t, tile_y[t : t + 1, :], wy)
    h, l = split(wy)
    wy_hi[...] = h
    wy_lo[...] = l

    def wx_of(shape, rows, reps_r, reps_c):
        r, c = iota(shape, 0), iota(shape, 1)
        t = r % wide - (HALO - QUARTER) - HALF * ((c % qx) // PATCH)
        t = jnp.where((r < wide * reps_r) & (c < qx * reps_c), t, -1)
        tile = jnp.dot(
            basis[1], (iota((PATCH, shape[1]), 0) == iota((PATCH, shape[1]), 1) % PATCH).astype(f32),
            precision=highest, preferred_element_type=f32,
        )
        w = jnp.zeros(shape, f32)
        for k in range(PATCH):
            w = jnp.where(t == k, tile[k : k + 1, :], w)
        return w

    pad_r = -(-2 * wide // LANES) * LANES
    pad_c = -(-qx // LANES) * LANES
    gx2 = wx_of((pad_r, pad_c), wide, 2, 1).T[:qx, : 2 * wide]
    g_hi, g_lo = split(gx2)
    g_lo = g_lo[:, :wide]
    b_hi, b_lo = split(wx_of((wide, 2 * qx), wide, 1, 2))
    b_lo = b_lo[:, :qx]

    c = iota((wide, 4 * wide), 1)
    dist_x = jnp.abs(iota((wide, 4 * wide), 0) - c % wide)
    bx = jnp.where(
        (c // wide) % 2 == 0,
        band_of(dist_x, [mass[1, k] for k in range(BAND + 1)]),
        band_of(dist_x, [stiff[1, k] for k in range(BAND + 1)]),
    )
    bx_hi, bx_lo = split(bx)
    bx_lo = bx_lo[:, : 2 * wide]

    lane_q = iota((1, qy), 1)
    cut = [cols[0, 0, m] for m in range(slots)]
    y_in = inner_y(iota((full, PATCH * PATCH), 0), ry)
    y_to = iota((full, PATCH * PATCH), 1) % PATCH
    for m in range(slots):
        b_m = cut[m] & (blocks_y - 1)
        sel[m] = (y_in + QUARTER - HALF * b_m == y_to).astype(f32).astype(bf16)

    def pick(shape, dim, row):
        index = iota(shape, dim)
        v = jnp.zeros(shape, f32)
        for k in range(PATCH):
            v = jnp.where(index % PATCH == k, values[row, k], v)
        return v

    lam = pick((qx, qy), 0, 1) + pick((qx, qy), 1, 2)
    column = (iota((qx, qy), 0) // PATCH) * blocks_y + iota((qx, qy), 1) // PATCH
    keep = jnp.ones((qx, qy), f32)
    for m in range(slots):
        keep = jnp.where(column == cut[m], 0.0, keep)
    for k in range(PATCH):
        dinv[k] = keep / (values[0, k] + lam)

    wait_recv_all(copy1)

    lane_w = iota((wide, LANES), 1)
    halo_l, halo_r = from_left[...], from_right[...]
    comb = jnp.where(lane_w < half, halo_l, pltpu.roll(halo_r, half, 1))
    low = lane_w % HALF < QUARTER
    load_t = jnp.where(low, halo_l, halo_r)
    act_t = jnp.where(low, pltpu.roll(halo_l, LANES - QUARTER, 1), pltpu.roll(halo_r, QUARTER, 1))
    act_w = ext[2 * nz]
    for z in range(nz):
        rows = pl.ds(z * wide, wide)
        h, l = split(ext[z])
        s_hi[rows, pl.ds(0, ry)] = h
        s_lo[rows, pl.ds(0, ry)] = l
        h, l = split(jnp.where((lane_w % half) // HALF == z, comb, 0.0))
        s_hi[rows, pl.ds(ry, LANES)] = h
        s_lo[rows, pl.ds(ry, LANES)] = l
    yv[...] = (
        dot(s_hi[...], yb_hi[...]) + dot(s_lo[...], yb_hi[...]) + dot(s_hi[...], yb_lo[...])
    ).reshape(nz, wide, 2 * full)

    def mix(step, carry):
        rows = pl.ds(pl.multiple_of(step * PATCH, PATCH), PATCH)
        y1 = [yv[z, rows, pl.ds(0, full)] for z in range(nz)]
        y2 = [yv[z, rows, pl.ds(full, full)] for z in range(nz)]
        for z in range(nz):
            p = q = None
            for w in range(nz):
                k = abs(z - w)
                if k > BAND:
                    continue
                m_y1 = mass[0, k] * y1[w]
                term = stiff[0, k] * y1[w] + mass[0, k] * y2[w]
                p = term if p is None else p + term
                q = m_y1 if q is None else q + m_y1
            for j, part in enumerate(split(p)):
                xpq[z, pl.ds(pl.multiple_of(2 * j * wide + step * PATCH, PATCH), PATCH), :] = part
            for j, part in enumerate(split(q)):
                xpq[z, pl.ds(pl.multiple_of((2 * j + 1) * wide + step * PATCH, PATCH), PATCH), :] = part
        return carry

    lax.fori_loop(0, wide // PATCH, mix, 0)

    for z in range(nz):
        applied = dot(bx_hi, xpq[z]) + dot(bx_lo, xpq[z, pl.ds(0, 2 * wide), :])
        rows = pl.ds(z * wide, wide)
        r0 = act_w * (ext[nz + z] - applied[:, :ry])
        mine = lane_w // HALF == half // HALF + z
        r1 = jnp.where(mine, act_t * (load_t - applied[:, ry:]), 0.0)
        h, l = split(r0)
        r_hi[rows, pl.ds(0, ry)] = h
        r_lo[rows, pl.ds(0, ry)] = l
        h, l = split(r1)
        r_hi[rows, pl.ds(ry, LANES)] = h
        r_lo[rows, pl.ds(ry, LANES)] = l

    t1 = dot(r_hi[...], wy_hi[...]) + dot(r_lo[...], wy_hi[...]) + dot(r_hi[...], wy_lo[...])
    for z in range(nz):
        h, l = split(t1[z * wide : (z + 1) * wide])
        uv[z] = dot(g_hi, jnp.concatenate([h, l], axis=0)) + dot(g_lo, h)

    def modes(step, carry):
        rows = pl.ds(pl.multiple_of(step * HALF, HALF), HALF)
        u = [uv[z, rows, :] for z in range(nz)]
        v = [None] * nz
        for k in range(PATCH):
            c = None
            for z in range(nz):
                term = basis_s[0, QUARTER + z, k] * u[z]
                c = term if c is None else c + term
            c = c * dinv[k, rows, :]
            for z in range(nz):
                term = basis_s[0, QUARTER + z, k] * c
                v[z] = term if v[z] is None else v[z] + term
        for z in range(nz):
            vv[z, rows, :] = v[z]
        return carry

    lax.fori_loop(0, qx // HALF, modes, 0)
    for z in range(nz):
        h, l = split(vv[z])
        back = dot(b_hi, jnp.concatenate([h, l], axis=0)) + dot(b_lo, h)
        h, l = split(back)
        tb_hi[pl.ds(z * wide, wide), :] = h
        tb_lo[pl.ds(z * wide, wide), :] = l

    total = (
        dot_nt(tb_hi[...], wy_hi[...]) + dot_nt(tb_lo[...], wy_hi[...]) + dot_nt(tb_hi[...], wy_lo[...])
    )

    fetch.wait()
    cells = PATCH * PATCH
    vz = basis[0, pl.ds(QUARTER, nz), :]
    cell_x = iota((wide, cells), 1) // PATCH
    row_k = iota((PATCH, cells), 0)
    for m in range(slots):
        a_m = cut[m] // blocks_y
        spot = (iota((wide, cells), 0) - (HALO - QUARTER) - HALF * a_m) == cell_x
        taken = (dot(r_hi[...], sel[m]) + dot(r_lo[...], sel[m])).reshape(nz, wide, cells)
        patch = jnp.sum(jnp.where(spot[None], taken, 0.0), axis=1)
        zmodes = lax.dot_general(
            vz, patch, (((0,), (0,)), ((), ())), precision=highest, preferred_element_type=f32
        ).astype(bf16)
        dense = jnp.zeros((PATCH, cells), f32)
        for k in range(PATCH):
            dense = jnp.where(row_k == k, dot_nt(zmodes, inv[m, k]), dense)
        corr = jnp.dot(vz, dense, precision=highest, preferred_element_type=f32)
        corr = jnp.where(cut[m] >= 0, corr, 0.0)
        spread = jnp.where(spot[None], corr[:, None, :], 0.0).reshape(nz * wide, cells)
        h, l = split(spread)
        total = total + dot_nt(h, sel[m]) + dot_nt(l, sel[m])

    total = total.reshape(nz, wide, full)
    packed = jnp.zeros((wide, LANES), f32)
    for z in range(nz):
        tot[z] = total[z, :, :ry]
        packed = jnp.where(lane_w // HALF == half // HALF + z, total[z, :, ry:], packed)
    edge[...] = packed

    start_all(copy2)
    wait_recv_all(copy2)

    lows = lane % HALF < QUARTER
    gap = jnp.zeros((rx - 2 * HALO, LANES), f32)
    l2 = left2[...] + jnp.concatenate([corners[0], gap, corners[2]], axis=0)
    r2 = right2[...] + jnp.concatenate([corners[1], gap, corners[3]], axis=0)
    both = jnp.where(lows, r2, l2)
    rim = (lane < QUARTER) | (lane >= ry - QUARTER)
    scale = damping * ext[2 * nz, own, :]
    for z in range(nz):
        moved = pltpu.roll(both, (LANES - QUARTER - half - HALF * z) % LANES, 1)
        t = tot[z, own, :] + jnp.concatenate([up[z], gap, down[z]], axis=0)
        t = t + jnp.where(rim, moved, 0.0)
        out[z] = state[z] + scale * t

    wait_send_all(copy1)
    wait_send_all(copy2)


def on_device(
    sizes, state, load_vector, active, stiff_band, mass_band, eig_basis, eig_values, cut_cols, cut_inverse
):
    nz, rx, ry = state.shape
    slots = cut_cols.shape[-1]
    assert nz == HALF and ry == LANES and rx % PATCH == 0
    inverse = cut_inverse.reshape(cut_inverse.shape[2:])
    wide = rx + 2 * HALO
    full = ry + LANES
    qx, qy = (rx // HALF) * PATCH, (ry // HALF) * PATCH
    cells = PATCH * PATCH
    vmem = pl.BlockSpec(memory_space=pltpu.VMEM)
    smem = pl.BlockSpec(memory_space=pltpu.SMEM)
    V = pltpu.VMEM
    dma = pltpu.SemaphoreType.DMA
    n = len(DIRS)
    return pl.pallas_call(
        functools.partial(kernel, sizes),
        out_shape=jax.ShapeDtypeStruct(state.shape, f32),
        in_specs=[vmem, vmem, vmem, smem, smem, smem, vmem, smem, smem, pl.BlockSpec(memory_space=pl.ANY)],
        out_specs=vmem,
        scratch_shapes=[
            V((2 * nz + 1, wide, ry), f32),
            V((wide, LANES), f32), V((wide, LANES), f32),
            V((rx, LANES), f32), V((rx, LANES), f32),
            V((slots, PATCH, cells, cells), bf16),
            V((full, 2 * full), bf16), V((full, 2 * full), bf16),
            V((full, qy), bf16), V((full, qy), bf16),
            V((slots, full, cells), bf16),
            V((PATCH, qx, qy), f32),
            V((nz * wide, full), bf16), V((nz * wide, full), bf16),
            V((nz, wide, 2 * full), f32),
            V((nz, 4 * wide, full), bf16),
            V((nz * wide, full), bf16), V((nz * wide, full), bf16),
            V((nz, qx, qy), f32), V((nz, qx, qy), f32),
            V((nz * wide, qy), bf16), V((nz * wide, qy), bf16),
            V((nz, wide, ry), f32), V((wide, LANES), f32),
            V((nz, HALO, ry), f32), V((nz, HALO, ry), f32),
            V((rx, LANES), f32), V((rx, LANES), f32),
            V((4, HALO, LANES), f32),
            dma, dma((n,)), dma((n,)), dma((n,)), dma((n,)),
        ],
        compiler_params=pltpu.CompilerParams(
            collective_id=0, has_side_effects=True, vmem_limit_bytes=40 * 1024 * 1024
        ),
    )(
        state, load_vector, active, stiff_band, mass_band, eig_basis, eig_basis, eig_values, cut_cols, inverse
    )


def solution(mesh):
    placed = (
        P(None, "gx", "gy"),
        P(None, "gx", "gy"),
        P("gx", "gy"),
        P(),
        P(),
        P(),
        P(),
        P("gx", "gy", None),
        P("gx", "gy", None, None, None, None),
    )
    sizes = (mesh.shape["gx"], mesh.shape["gy"])
    return jax.shard_map(
        functools.partial(on_device, sizes),
        mesh=mesh, in_specs=placed, out_specs=P(None, "gx", "gy"), check_vma=False,
    )
```

time: 155 us -> 28.9 us (0.19)
  local copies, waits for them, and re-layouts: 60 us -> 8.74 us
  other arithmetic: 47.7 us -> 0 us
  starting transfers between devices: 22.5 us -> 0 us
  Pallas kernels: 0 us -> 19.8 us
  waiting for transfers between devices: 14.7 us -> 0 us
  matrix products: 8.68 us -> 0 us
    add x9 -> x0, other arithmetic: 27.7 us -> none  [the longest x3 10 us: fold_blocks(): return jnp.pad(lower, widths_low) + jnp.pad(upper, widths_high)]
    slice x14 -> x0, local copies, waits for them, and re-layouts: 22.5 us -> none  [the longest x5 11.7 us: on_device(): blocks = jnp.concatenate([blocks[:-1], blocks[1:]], axis=1)]
    ppermute x8 -> x0, starting transfers between devices: 22.5 us -> none  [the longest x4 14.6 us: with_halo(): before = lax.ppermute(last, axis, up)]
    pallas_call x0 -> x1, Pallas kernels: none -> 19.8 us  [on_device(): pl.pallas_call(functools.partial(kernel, sizes), out_shape=jax.ShapeDtype...]
    reshape x3 -> x0, local copies, waits for them, and re-layouts: 17.6 us -> none  [the longest x2 12.9 us: on_device(): merged.reshape(blocks_z, PATCH, blocks_x, blocks_y, PATCH, PATCH)]
    ppermute x8 -> x0, waiting for transfers between devices: 14.7 us -> none  [the longest x4 12.4 us: with_halo(): after = lax.ppermute(initial, axis, down)]
    transpose x1 -> x0, local copies, waits for them, and re-layouts: 10.7 us -> none  [on_device(): blocks.transpose(0, 1, 2, 4, 3, 5)]
    mul x4 -> x0, other arithmetic: 9.76 us -> none  [the longest x2 9.55 us: on_device(): resid_ext = inner[depth][None] * (inner[:depth] - applied)]
  transfers between devices with their start and end apart: 8 -> 0, of which waited for: 5 -> 0; matrix products, arithmetic and copies ran while one was open for 4% -> 0% of each run, Pallas kernels for 0% -> 0%
where the time goes in v1:
time: 28.9 us; the launch traced here: 28.5 us
  Pallas kernels  19.8 us (69%)
  local copies, waits for them, and re-layouts  8.74 us (30%)
    pallas_call x1, Pallas kernels, on_device(): pl.pallas_call(functools.partial(kernel, sizes), out_shape=jax.ShapeDtype...  19.8 us
    unnamed x19, local copies, waits for them, and re-layouts  8.74 us

profile of v1, /device:TPU:13, one launch (start us, length us, event | category | flops | bytes accessed | tf_op | source)
XLA Modules:
  0.0 28.5 jit_solution(435852297384809415)
XLA Ops:
  0.0 0.0 copy-start
  0.0 2.2 %copy-done = bf16[1,1,2,16,256,256]{5,4,3,2,1,0:T(8,128)(2,1)S(1)} copy-done((bf16[1,1,2,16,256,256]{5,4,3,2,1,0:T(8,128)(2,1)S(1)}, bf16[1,1,2,16,256,256]{5,4,3,2,1,0:T(8,128)(2,1)}, u32[]{:S(2)}) %copy-start) | copy-done | bytes 4194328
  2.2 0.0 copy-start.1
  2.2 0.9 %copy-done.1 = f32[8,32,128]{2,1,0:T(8,128)S(1)} copy-done((f32[8,32,128]{2,1,0:T(8,128)S(1)}, f32[8,32,128]{2,1,0:T(8,128)}, u32[]{:S(2)}) %copy-start.1) | copy-done | bytes 131096
  3.1 0.0 copy-start.2
  3.1 0.7 %copy-done.2 = f32[3,16,16]{2,1,0:T(8,128)S(1)} copy-done((f32[3,16,16]{2,1,0:T(8,128)S(1)}, f32[3,16,16]{2,1,0:T(8,128)}, u32[]{:S(2)}) %copy-start.2) | copy-done | bytes 3096
  3.8 0.0 copy-start.3
  3.8 0.8 %copy-done.3 = bf16[8,32,128]{2,1,0:T(8,128)(2,1)S(1)} copy-done((bf16[8,32,128]{2,1,0:T(8,128)(2,1)S(1)}, bf16[8,32,128]{2,1,0:T(8,128)(2,1)}, u32[]{:S(2)}) %copy-start.3) | copy-done | bytes 65560
  4.7 0.0 copy-start.4
  4.7 0.7 %copy-done.4 = s32[32,128]{1,0:T(8,128)S(1)} copy-done((s32[32,128]{1,0:T(8,128)S(1)}, s32[32,128]{1,0:T(8,128)}, u32[]{:S(2)}) %copy-start.4) | copy-done | bytes 16408
  5.4 0.0 copy-start.5
  5.4 0.7 %copy-done.5 = f32[3,5]{1,0:T(4,128)S(1)} copy-done((f32[3,5]{1,0:T(4,128)S(1)}, f32[3,5]{1,0:T(4,128)}, u32[]{:S(2)}) %copy-start.5) | copy-done | bytes 84
  6.1 0.0 copy-start.6
  6.1 0.7 %copy-done.6 = f32[3,5]{1,0:T(4,128)S(1)} copy-done((f32[3,5]{1,0:T(4,128)S(1)}, f32[3,5]{1,0:T(4,128)}, u32[]{:S(2)}) %copy-start.6) | copy-done | bytes 84
  6.8 0.0 copy-start.7
  6.8 0.7 %copy-done.7 = f32[3,16]{1,0:T(4,128)S(1)} copy-done((f32[3,16]{1,0:T(4,128)S(1)}, f32[3,16]{1,0:T(4,128)}, u32[]{:S(2)}) %copy-start.7) | copy-done | bytes 216
  7.4 0.0 copy-start.8
  7.4 0.7 %copy-done.8 = s32[1,1,2]{2,1,0:T(1,128)S(1)} copy-done((s32[1,1,2]{2,1,0:T(1,128)S(1)}, s32[1,1,2]{2,1,0:T(1,128)}, u32[]{:S(2)}) %copy-start.8) | copy-done | bytes 32
  8.1 19.8 %shard_map.91 = f32[8,32,128]{2,1,0:T(8,128)S(1)} custom-call(f32[8,32,128]{2,1,0:T(8,128)S(1)} %copy-done.1, bf16[8,32,128]{2,1,0:T(8,128)(2,1)S(1)} %copy-done.3, s32[32,128]{1,0:T(8,128)S(1)} %copy-done.4, f32[3,5]{1,0:T(4,128)S(1)} %copy-done.5, f32[3,5]{1,0:T(4,128)S(1)} %copy-done.6, f32[3,16,16]{2,1,0:T(8,128)S(1)} %copy-done.2, ...), custom_call_target="tpu_custom_call" | custom-call | tf_op jit(solution)/shard_map/pallas_call | solution.py:416
  27.9 0.7 %copy.11 = f32[8,32,128]{2,1,0:T(8,128)} copy(f32[8,32,128]{2,1,0:T(8,128)S(1)} %shard_map.91) | data formatting | bytes 262144
Async XLA Ops:
  0.0 2.2 %copy-start = (bf16[1,1,2,16,256,256]{5,4,3,2,1,0:T(8,128)(2,1)S(1)}, bf16[1,1,2,16,256,256]{5,4,3,2,1,0:T(8,128)(2,1)}, u32[]{:S(2)}) copy-start(bf16[1,1,2,16,256,256]{5,4,3,2,1,0:T(8,128)(2,1)} %param.17) | copy-start | bytes 12582916
  2.2 0.9 %copy-start.1 = (f32[8,32,128]{2,1,0:T(8,128)S(1)}, f32[8,32,128]{2,1,0:T(8,128)}, u32[]{:S(2)}) copy-start(f32[8,32,128]{2,1,0:T(8,128)} %state.1) | copy-start | bytes 393220
  3.1 0.7 %copy-start.2 = (f32[3,16,16]{2,1,0:T(8,128)S(1)}, f32[3,16,16]{2,1,0:T(8,128)}, u32[]{:S(2)}) copy-start(f32[3,16,16]{2,1,0:T(8,128)} %basis.1) | copy-start | bytes 9220
  3.8 0.8 %copy-start.3 = (bf16[8,32,128]{2,1,0:T(8,128)(2,1)S(1)}, bf16[8,32,128]{2,1,0:T(8,128)(2,1)}, u32[]{:S(2)}) copy-start(bf16[8,32,128]{2,1,0:T(8,128)(2,1)} %load.1) | copy-start | bytes 196612
  4.7 0.7 %copy-start.4 = (s32[32,128]{1,0:T(8,128)S(1)}, s32[32,128]{1,0:T(8,128)}, u32[]{:S(2)}) copy-start(s32[32,128]{1,0:T(8,128)} %active.1) | copy-start | bytes 49156
  5.4 0.7 %copy-start.5 = (f32[3,5]{1,0:T(4,128)S(1)}, f32[3,5]{1,0:T(4,128)}, u32[]{:S(2)}) copy-start(f32[3,5]{1,0:T(4,128)} %stiff.1) | copy-start | bytes 184
  6.1 0.7 %copy-start.6 = (f32[3,5]{1,0:T(4,128)S(1)}, f32[3,5]{1,0:T(4,128)}, u32[]{:S(2)}) copy-start(f32[3,5]{1,0:T(4,128)} %mass.1) | copy-start | bytes 184
  6.8 0.7 %copy-start.7 = (f32[3,16]{1,0:T(4,128)S(1)}, f32[3,16]{1,0:T(4,128)}, u32[]{:S(2)}) copy-start(f32[3,16]{1,0:T(4,128)} %values.1) | copy-start | bytes 580
  7.4 0.7 %copy-start.8 = (s32[1,1,2]{2,1,0:T(1,128)S(1)}, s32[1,1,2]{2,1,0:T(1,128)}, u32[]{:S(2)}) copy-start(s32[1,1,2]{2,1,0:T(1,128)} %cols.1) | copy-start | bytes 28

commit v2 on v1

v2 whole, which is shorter than its diff:
```python
import functools

import jax
import jax.numpy as jnp
from jax import lax
from jax.experimental import pallas as pl
from jax.experimental.pallas import tpu as pltpu
from jax.sharding import PartitionSpec as P

BAND = 4
PATCH = 16
HALF = PATCH // 2
QUARTER = PATCH // 4
HALO = BAND + QUARTER
LANES = 128
MESH = pl.DeviceIdType.MESH
DIRS = [(dx, dy) for dx in (-1, 0, 1) for dy in (-1, 0, 1) if (dx, dy) != (0, 0)]

damping = 0.5
f32 = jnp.float32
bf16 = jnp.bfloat16


def iota(shape, dim):
    return lax.broadcasted_iota(jnp.int32, shape, dim)


def split(v):
    hi = v.astype(bf16)
    return hi, (v - hi.astype(f32)).astype(bf16)


def dot(a, b):
    return jnp.dot(a, b, preferred_element_type=f32)


def dot_nt(a, b):
    return lax.dot_general(a, b, (((1,), (1,)), ((), ())), preferred_element_type=f32)


def band_of(distance, taps):
    out = jnp.zeros(distance.shape, f32)
    for k in range(BAND + 1):
        out = jnp.where(distance == k, taps[k], out)
    return out


def inner_y(c, ry):
    u = (c - ry) & (HALF - 1)
    halo = jnp.where(u < QUARTER, u - QUARTER, ry + u - QUARTER)
    return jnp.where(c < ry, c, jnp.where(c < ry + LANES // 2, -1000, halo))


def outer_y(r, ry):
    u = (r - ry) & (HALF - 1)
    return jnp.where(r < ry, r, jnp.where(r < ry + LANES // 2, u - HALO, ry + u))


def wrap(v, n, reps):
    out = v
    for j in range(1, reps):
        out = out - jnp.where(v >= n * j, n, 0)
    return out


def kernel(
    sizes,
    state_h, load_h, active_h, stiff_h, mass_h, basis_h, values_h, cols_h, inverse_h,
    out,
    state, load, active, stiff, mass, basis_s, basis, values, cols, inv,
    ext, from_left, from_right, pack_left, pack_right,
    yb_hi, yb_lo, wy_hi, wy_lo, sel, dinv,
    zk, zm, sk_hi, sk_lo, sm_hi, sm_lo, r_hi, r_lo, tb_hi, tb_lo, tot, edge,
    up, down, left2, right2, corners,
    in_sem, send1, recv1, send2, recv2,
):
    n_x, n_y = sizes
    nz, rx, ry = state.shape
    wide = rx + 2 * HALO
    slots = inv.shape[0]
    blocks_x, blocks_y = rx // HALF, ry // HALF
    qx, qy = blocks_x * PATCH, blocks_y * PATCH
    full = ry + LANES
    half = LANES // 2
    groups = half // HALF
    me_x, me_y = lax.axis_index("gx"), lax.axis_index("gy")

    def exists(dx, dy):
        ok = None
        for d, me, n in ((dx, me_x, n_x), (dy, me_y, n_y)):
            if d:
                part = (me + d >= 0) & (me + d < n)
                ok = part if ok is None else ok & part
        return ok

    def device(dx, dy):
        return (jnp.clip(me_x + dx, 0, n_x - 1), jnp.clip(me_y + dy, 0, n_y - 1))

    fetches = [
        pltpu.make_async_copy(src, dst, in_sem.at[i])
        for i, (src, dst) in enumerate((
            (state_h, state), (load_h, load), (active_h, active),
            (stiff_h, stiff), (mass_h, mass), (basis_h, basis_s), (basis_h, basis),
            (values_h, values), (cols_h, cols), (inverse_h, inv),
        ))
    ]
    for fetch in fetches:
        fetch.start()

    own = pl.ds(HALO, rx)
    zeros = jnp.zeros((2 * nz + 1, HALO, ry), f32)
    ext[:, pl.ds(0, HALO), :] = zeros
    ext[:, pl.ds(HALO + rx, HALO), :] = zeros
    for ref in (from_left, from_right, up, down, left2, right2, corners):
        ref[...] = jnp.zeros(ref.shape, f32)

    barrier = pltpu.get_barrier_semaphore()
    count = jnp.int32(0)
    for d in DIRS:
        ok = exists(*d)
        count = count + ok.astype(jnp.int32)

        @pl.when(ok)
        def _(d=d):
            pl.semaphore_signal(barrier, inc=1, device_id=device(*d), device_id_type=MESH)

    for fetch in fetches[:3]:
        fetch.wait()
    for z in range(nz):
        ext[z, own, :] = state[z]
        ext[nz + z, own, :] = load[z].astype(f32)
    ext[2 * nz, own, :] = active[...].astype(f32)

    lane = iota((rx, LANES), 1)
    group = (lane & (half - 1)) >> 3
    high = lane >= half
    lows = (lane & (HALF - 1)) < QUARTER
    to_right = jnp.zeros((rx, LANES), f32)
    to_left = jnp.zeros((rx, LANES), f32)
    act = ext[2 * nz, own, :]
    for z in range(nz):
        s = ext[z, own, :]
        l = pltpu.roll(ext[nz + z, own, :], (half + QUARTER + HALF * z) % LANES, 1)
        mine = group == z
        first = mine & high & lows
        second = mine & high & ~lows
        to_right = jnp.where(mine & ~high, pltpu.roll(s, (HALF + HALF * z) % LANES, 1), to_right)
        to_right = jnp.where(first, l, to_right)
        to_right = jnp.where(second, pltpu.roll(act, (half + HALF + HALF * z) % LANES, 1), to_right)
        to_left = jnp.where(mine & ~high, pltpu.roll(s, HALF * z, 1) if z else s, to_left)
        to_left = jnp.where(second, l, to_left)
        to_left = jnp.where(first, pltpu.roll(act, (half + HALF * z) % LANES, 1), to_left)
    pack_right[...] = to_right
    pack_left[...] = to_left

    def copy1(i):
        dx, dy = DIRS[i]
        if dy == 0:
            src = ext.at[:, pl.ds(rx if dx > 0 else HALO, HALO), :]
            dst = ext.at[:, pl.ds(0 if dx > 0 else HALO + rx, HALO), :]
        else:
            pack = pack_right if dy > 0 else pack_left
            land = from_left if dy > 0 else from_right
            if dx == 0:
                src, dst = pack, land.at[pl.ds(HALO, rx), :]
            else:
                src = pack.at[pl.ds(rx - HALO if dx > 0 else 0, HALO), :]
                dst = land.at[pl.ds(0 if dx > 0 else HALO + rx, HALO), :]
        return pltpu.make_async_remote_copy(
            src_ref=src, dst_ref=dst, send_sem=send1.at[i], recv_sem=recv1.at[i],
            device_id=device(dx, dy), device_id_type=MESH,
        )

    def copy2(i):
        dx, dy = DIRS[i]
        if dy == 0:
            src = tot.at[:, pl.ds(HALO + rx if dx > 0 else 0, HALO), :]
            dst = up if dx > 0 else down
        elif dx == 0:
            src = edge.at[pl.ds(HALO, rx), :]
            dst = left2 if dy > 0 else right2
        else:
            src = edge.at[pl.ds(HALO + rx if dx > 0 else 0, HALO), :]
            dst = corners.at[(dx < 0) * 2 + (dy < 0)]
        return pltpu.make_async_remote_copy(
            src_ref=src, dst_ref=dst, send_sem=send2.at[i], recv_sem=recv2.at[i],
            device_id=device(dx, dy), device_id_type=MESH,
        )

    def start_all(copy):
        for i, d in enumerate(DIRS):
            @pl.when(exists(*d))
            def _(i=i):
                copy(i).start()

    def wait_recv_all(copy):
        for i, (dx, dy) in enumerate(DIRS):
            @pl.when(exists(-dx, -dy))
            def _(i=i):
                copy(i).wait_recv()

    def wait_send_all(copy):
        for i, d in enumerate(DIRS):
            @pl.when(exists(*d))
            def _(i=i):
                copy(i).wait_send()

    pl.semaphore_wait(barrier, count)
    start_all(copy1)

    for fetch in fetches[3:9]:
        fetch.wait()
    distance = jnp.abs(outer_y(iota((full, 1), 0), ry) - inner_y(iota((1, full), 1), ry))
    for j, taps in enumerate((mass, stiff)):
        h, l = split(band_of(distance, [taps[2, k] for k in range(BAND + 1)]))
        yb_hi[:, pl.ds(j * full, full)] = h
        yb_lo[:, pl.ds(j * full, full)] = l

    highest = lax.Precision.HIGHEST
    tile_y = jnp.dot(
        basis[2], (iota((PATCH, qy), 0) == (iota((PATCH, qy), 1) & (PATCH - 1))).astype(f32),
        precision=highest, preferred_element_type=f32,
    )
    place = inner_y(iota((full, 1), 0), ry) + QUARTER - HALF * (iota((1, qy), 1) >> 4)
    wy = jnp.zeros((full, qy), f32)
    for t in range(PATCH):
        wy = jnp.where(place == t, tile_y[t : t + 1, :], wy)
    h, l = split(wy)
    wy_hi[...] = h
    wy_lo[...] = l

    def wx_of(shape, reps_r, reps_c):
        r, c = iota((shape[0], 1), 0), iota((1, shape[1]), 1)
        t = wrap(r, wide, reps_r) - (HALO - QUARTER) - HALF * (wrap(c, qx, reps_c) >> 4)
        t = jnp.where((r < wide * reps_r) & (c < qx * reps_c), t, -1)
        tile = jnp.dot(
            basis[1], (iota((PATCH, shape[1]), 0) == (iota((PATCH, shape[1]), 1) & (PATCH - 1))).astype(f32),
            precision=highest, preferred_element_type=f32,
        )
        w = jnp.zeros(shape, f32)
        for k in range(PATCH):
            w = jnp.where(t == k, tile[k : k + 1, :], w)
        return w

    pad_r = -(-2 * wide // LANES) * LANES
    pad_c = -(-qx // LANES) * LANES
    gx2 = wx_of((pad_r, pad_c), 2, 1).T[:qx, : 2 * wide]
    g_hi, g_lo = split(gx2)
    g_lo = g_lo[:, :wide]
    b_hi, b_lo = split(wx_of((wide, 2 * qx), 1, 2))
    b_lo = b_lo[:, :qx]

    c = iota((1, 4 * wide), 1)
    dist_x = jnp.abs(iota((wide, 1), 0) - wrap(c, wide, 4))
    bx = jnp.where(
        (c < wide) | ((c >= 2 * wide) & (c < 3 * wide)),
        band_of(dist_x, [mass[1, k] for k in range(BAND + 1)]),
        band_of(dist_x, [stiff[1, k] for k in range(BAND + 1)]),
    )
    bx_hi, bx_lo = split(bx)
    bx_lo = bx_lo[:, : 2 * wide]

    cells = PATCH * PATCH
    cut = [cols[0, 0, m] for m in range(slots)]
    cut_a = [lax.div(jnp.maximum(v, 0), jnp.int32(blocks_y)) for v in cut]
    cut_b = [lax.rem(jnp.maximum(v, 0), jnp.int32(blocks_y)) for v in cut]
    y_in = inner_y(iota((full, 1), 0), ry)
    y_to = iota((1, cells), 1) & (PATCH - 1)
    for m in range(slots):
        sel[m] = jnp.where(y_in + QUARTER - HALF * cut_b[m] == y_to, 1.0, 0.0).astype(bf16)

    def pick(shape, dim, row):
        index = iota(shape, dim) & (PATCH - 1)
        v = jnp.zeros(shape, f32)
        for k in range(PATCH):
            v = jnp.where(index == k, values[row, k], v)
        return v

    lam = pick((qx, 1), 0, 1) + pick((1, qy), 1, 2)
    column = (iota((qx, 1), 0) >> 4) * blocks_y + (iota((1, qy), 1) >> 4)
    keep = jnp.ones((qx, qy), f32)
    for m in range(slots):
        keep = jnp.where(column == cut[m], 0.0, keep)
    for k in range(PATCH):
        dinv[k] = keep / (values[0, k] + lam)

    lane1 = iota((1, LANES), 1)
    group1 = (lane1 & (half - 1)) >> 3
    far = [jnp.abs(group1 - z) for z in range(nz)]
    k_vec = [band_of(far[z], [stiff[0, k] for k in range(BAND + 1)]) for z in range(nz)]
    m_vec = [band_of(far[z], [mass[0, k] for k in range(BAND + 1)]) for z in range(nz)]
    v_vec = []
    for k in range(PATCH):
        v = jnp.zeros((1, LANES), f32)
        for z in range(nz):
            v = jnp.where((group1 == z) & (lane1 >= half), basis_s[0, QUARTER + z, k], v)
        v_vec.append(v)

    def mix_z(start, count):
        for r in range(start, start + count, HALF):
            rows = pl.ds(r, HALF)
            s = [ext[z, rows, :] for z in range(nz)]
            for z in range(nz):
                p = q = None
                for w in range(nz):
                    k = abs(z - w)
                    if k > BAND:
                        continue
                    a, b = stiff[0, k] * s[w], mass[0, k] * s[w]
                    p = a if p is None else p + a
                    q = b if q is None else q + b
                zk[z, rows, :] = p
                zm[z, rows, :] = q

    mix_z(HALO, rx)
    wait_recv_all(copy1)
    mix_z(0, HALO)
    mix_z(HALO + rx, HALO)

    lane_w = iota((wide, LANES), 1)
    group_w = (lane_w & (half - 1)) >> 3
    halo_l, halo_r = from_left[...], from_right[...]
    comb = jnp.where(lane_w < half, halo_l, pltpu.roll(halo_r, half, 1))
    low = (lane_w & (HALF - 1)) < QUARTER
    load_t = jnp.where(low, halo_l, halo_r)
    act_t = jnp.where(low, pltpu.roll(halo_l, LANES - QUARTER, 1), pltpu.roll(halo_r, QUARTER, 1))
    act_t = jnp.where(lane_w >= half, act_t, 0.0)
    act_w = ext[2 * nz]
    for z in range(nz):
        rows = pl.ds(z * wide, wide)
        for hi, lo, mixed, vec in ((sk_hi, sk_lo, zk, k_vec), (sm_hi, sm_lo, zm, m_vec)):
            h, l = split(mixed[z])
            hi[rows, pl.ds(0, ry)] = h
            lo[rows, pl.ds(0, ry)] = l
            h, l = split(comb * vec[z])
            hi[rows, pl.ds(ry, LANES)] = h
            lo[rows, pl.ds(ry, LANES)] = l

    def times(hi, lo, w_hi, w_lo):
        return dot(hi, w_hi) + dot(lo, w_hi) + dot(hi, w_lo)

    ym = times(sm_hi[...], sm_lo[...], yb_hi[...], yb_lo[...])
    yp = ym[:, full:] + times(sk_hi[...], sk_lo[...], yb_hi[:, pl.ds(0, full)], yb_lo[:, pl.ds(0, full)])

    r0 = []
    r1 = jnp.zeros((wide, LANES), f32)
    for z in range(nz):
        p_hi, p_lo = split(yp[z * wide : (z + 1) * wide])
        q_hi, q_lo = split(ym[z * wide : (z + 1) * wide, :full])
        applied = dot(bx_hi, jnp.concatenate([p_hi, q_hi, p_lo, q_lo], axis=0))
        applied = applied + dot(bx_lo, jnp.concatenate([p_hi, q_hi], axis=0))
        r0.append(act_w * (ext[nz + z] - applied[:, :ry]))
        r1 = jnp.where(group_w == z, applied[:, ry:], r1)
    r1 = act_t * (load_t - r1)

    for k in range(PATCH):
        rows = pl.ds(k * wide, wide)
        v = None
        for z in range(nz):
            term = basis_s[0, QUARTER + z, k] * r0[z]
            v = term if v is None else v + term
        h, l = split(v)
        r_hi[rows, pl.ds(0, ry)] = h
        r_lo[rows, pl.ds(0, ry)] = l
        h, l = split(r1 * v_vec[k])
        r_hi[rows, pl.ds(ry, LANES)] = h
        r_lo[rows, pl.ds(ry, LANES)] = l

    fetches[9].wait()
    vz = basis[0, pl.ds(QUARTER, nz), :]
    cell_x = iota((1, cells), 1) >> 4
    row_k = iota((PATCH, cells), 0)
    spread = []
    for m in range(slots):
        spot = (iota((wide, 1), 0) - (HALO - QUARTER) - HALF * cut_a[m]) == cell_x
        taken = (dot(r_hi[...], sel[m]) + dot(r_lo[...], sel[m])).reshape(PATCH, wide, cells)
        zmodes = jnp.sum(jnp.where(spot[None], taken, 0.0), axis=1).astype(bf16)
        dense = jnp.zeros((PATCH, cells), f32)
        for k in range(PATCH):
            dense = jnp.where(row_k == k, dot_nt(zmodes, inv[m, k]), dense)
        corr = jnp.dot(vz, dense, precision=highest, preferred_element_type=f32)
        corr = jnp.where(cut[m] >= 0, corr, 0.0)
        spread.append(jnp.where(spot[None], corr[:, None, :], 0.0).reshape(nz * wide, cells))

    t1 = times(r_hi[...], r_lo[...], wy_hi[...], wy_lo[...])
    for k in range(PATCH):
        h, l = split(t1[k * wide : (k + 1) * wide])
        u = (dot(g_hi, jnp.concatenate([h, l], axis=0)) + dot(g_lo, h)) * dinv[k]
        h, l = split(u)
        back = dot(b_hi, jnp.concatenate([h, l], axis=0)) + dot(b_lo, h)
        h, l = split(back)
        tb_hi[pl.ds(k * wide, wide), :] = h
        tb_lo[pl.ds(k * wide, wide), :] = l
    fast = (
        dot_nt(tb_hi[...], wy_hi[...]) + dot_nt(tb_lo[...], wy_hi[...]) + dot_nt(tb_hi[...], wy_lo[...])
    ).reshape(PATCH, wide, full)

    cut_total = None
    for m in range(slots):
        h, l = split(spread[m])
        term = dot_nt(h, sel[m]) + dot_nt(l, sel[m])
        cut_total = term if cut_total is None else cut_total + term
    cut_total = cut_total.reshape(nz, wide, full)

    packed = jnp.zeros((wide, LANES), f32)
    for z in range(nz):
        packed = jnp.where(group_w == z, cut_total[z, :, ry:], packed)
    for k in range(PATCH):
        packed = packed + v_vec[k] * fast[k, :, ry:]
    edge[...] = packed
    for z in range(nz):
        t = cut_total[z, :, :ry]
        for k in range(PATCH):
            t = t + basis_s[0, QUARTER + z, k] * fast[k, :, :ry]
        tot[z] = t

    start_all(copy2)
    wait_recv_all(copy2)

    gap = jnp.zeros((rx - 2 * HALO, LANES), f32)
    l2 = left2[...] + jnp.concatenate([corners[0], gap, corners[2]], axis=0)
    r2 = right2[...] + jnp.concatenate([corners[1], gap, corners[3]], axis=0)
    both = jnp.where(lows, r2, l2)
    rim = (lane < QUARTER) | (lane >= ry - QUARTER)
    scale = damping * ext[2 * nz, own, :]
    for z in range(nz):
        moved = pltpu.roll(both, (LANES - QUARTER - half - HALF * z) % LANES, 1)
        t = tot[z, own, :] + jnp.concatenate([up[z], gap, down[z]], axis=0)
        t = t + jnp.where(rim, moved, 0.0)
        out[z] = state[z] + scale * t

    wait_send_all(copy1)
    wait_send_all(copy2)


def on_device(
    sizes, state, load_vector, active, stiff_band, mass_band, eig_basis, eig_values, cut_cols, cut_inverse
):
    nz, rx, ry = state.shape
    slots = cut_cols.shape[-1]
    assert nz == HALF and ry == LANES and rx % PATCH == 0
    inverse = cut_inverse.reshape(cut_inverse.shape[2:])
    wide = rx + 2 * HALO
    full = ry + LANES
    qx, qy = (rx // HALF) * PATCH, (ry // HALF) * PATCH
    cells = PATCH * PATCH
    anyspace = pl.BlockSpec(memory_space=pl.ANY)
    V, S = pltpu.VMEM, pltpu.SMEM
    dma = pltpu.SemaphoreType.DMA
    n = len(DIRS)
    return pl.pallas_call(
        functools.partial(kernel, sizes),
        out_shape=jax.ShapeDtypeStruct(state.shape, f32),
        in_specs=[anyspace] * 9,
        out_specs=pl.BlockSpec(memory_space=pltpu.VMEM),
        scratch_shapes=[
            V(state.shape, f32), V(load_vector.shape, load_vector.dtype), V(active.shape, active.dtype),
            S(stiff_band.shape, f32), S(mass_band.shape, f32), S(eig_basis.shape, f32),
            V(eig_basis.shape, f32), S(eig_values.shape, f32), S(cut_cols.shape, cut_cols.dtype),
            V((slots, PATCH, cells, cells), bf16),
            V((2 * nz + 1, wide, ry), f32),
            V((wide, LANES), f32), V((wide, LANES), f32),
            V((rx, LANES), f32), V((rx, LANES), f32),
            V((full, 2 * full), bf16), V((full, 2 * full), bf16),
            V((full, qy), bf16), V((full, qy), bf16),
            V((slots, full, cells), bf16),
            V((PATCH, qx, qy), f32),
            V((nz, wide, ry), f32), V((nz, wide, ry), f32),
            V((nz * wide, full), bf16), V((nz * wide, full), bf16),
            V((nz * wide, full), bf16), V((nz * wide, full), bf16),
            V((PATCH * wide, full), bf16), V((PATCH * wide, full), bf16),
            V((PATCH * wide, qy), bf16), V((PATCH * wide, qy), bf16),
            V((nz, wide, ry), f32), V((wide, LANES), f32),
            V((nz, HALO, ry), f32), V((nz, HALO, ry), f32),
            V((rx, LANES), f32), V((rx, LANES), f32),
            V((4, HALO, LANES), f32),
            dma((10,)), dma((n,)), dma((n,)), dma((n,)), dma((n,)),
        ],
        compiler_params=pltpu.CompilerParams(
            collective_id=0, has_side_effects=True, vmem_limit_bytes=56 * 1024 * 1024
        ),
    )(state, load_vector, active, stiff_band, mass_band, eig_basis, eig_values, cut_cols, inverse)


def solution(mesh):
    placed = (
        P(None, "gx", "gy"),
        P(None, "gx", "gy"),
        P("gx", "gy"),
        P(),
        P(),
        P(),
        P(),
        P("gx", "gy", None),
        P("gx", "gy", None, None, None, None),
    )
    sizes = (mesh.shape["gx"], mesh.shape["gy"])
    return jax.shard_map(
        functools.partial(on_device, sizes),
        mesh=mesh, in_specs=placed, out_specs=P(None, "gx", "gy"), check_vma=False,
    )
```

time: 28.9 us -> 22 us (0.76)
  local copies, waits for them, and re-layouts: 8.74 us -> 1.57 us
  Pallas kernels: 19.8 us -> 20.3 us
    unnamed x19 -> x1, local copies, waits for them, and re-layouts: 8.74 us -> 1.57 us
    pallas_call x1, Pallas kernels: 19.8 us -> 20.3 us  [on_device(): pl.pallas_call(functools.partial(kernel, sizes), out_shape=jax.ShapeDtype...]
where the time goes in v2:
time: 22 us; the launch traced here: 21.8 us
  Pallas kernels  20.3 us (92%)
  local copies, waits for them, and re-layouts  1.57 us (7%)
    pallas_call x1, Pallas kernels, on_device(): pl.pallas_call(functools.partial(kernel, sizes), out_shape=jax.ShapeDtype...  20.3 us
    unnamed x1, local copies, waits for them, and re-layouts  1.57 us

profile of v2, /device:TPU:13, one launch (start us, length us, event | category | flops | bytes accessed | tf_op | source)
XLA Modules:
  0.0 21.8 jit_solution(17073273835729738911)
XLA Ops:
  0.0 20.3 %shard_map.91 = f32[8,32,128]{2,1,0:T(8,128)} custom-call(f32[8,32,128]{2,1,0:T(8,128)} %state_h.1, bf16[8,32,128]{2,1,0:T(8,128)(2,1)} %load_h.1, s32[32,128]{1,0:T(8,128)} %active_h.1, f32[3,5]{1,0:T(4,128)} %stiff_h.1, f32[3,5]{1,0:T(4,128)} %mass_h.1, f32[3,16,16]{2,1,0:T(8,128)} %basis_h.1, f32[3,16]{1,0:T(4,128)} %values_h.1, s32[1,1,2]{2,1,0:T(1,128)} %cols_h.1, ...), custom_call_target="tpu_custom_call" | custom-call | tf_op jit(solution)/shard_map/pallas_call | solution.py:451
  20.3 1.6 %copy.11 = f32[8,32,128]{2,1,0:T(8,128)} copy(f32[8,32,128]{2,1,0:T(8,128)} %shard_map.91) | data formatting | bytes 262144

commit v3 on v2

--- a/solution.py
+++ b/solution.py
@@ -14,7 +14,7 @@
 HALO = BAND + QUARTER
 LANES = 128
 MESH = pl.DeviceIdType.MESH
-DIRS = [(dx, dy) for dx in (-1, 0, 1) for dy in (-1, 0, 1) if (dx, dy) != (0, 0)]
+DIRS = [(1, 0), (-1, 0), (1, 1), (1, -1), (-1, 1), (-1, -1), (0, 1), (0, -1)]
 
 damping = 0.5
 f32 = jnp.float32
@@ -68,10 +68,10 @@
     state_h, load_h, active_h, stiff_h, mass_h, basis_h, values_h, cols_h, inverse_h,
     out,
     state, load, active, stiff, mass, basis_s, basis, values, cols, inv,
-    ext, from_left, from_right, pack_left, pack_right,
-    yb_hi, yb_lo, wy_hi, wy_lo, sel, dinv,
-    zk, zm, sk_hi, sk_lo, sm_hi, sm_lo, r_hi, r_lo, tb_hi, tb_lo, tot, edge,
-    up, down, left2, right2, corners,
+    ext, lf, from_left, from_right, pack_left, pack_right,
+    yb, wy3, wyt3, sel, dinv,
+    zk, zm, sk3, sm3, r3, tb3, tot, edge,
+    rim_x, up, down, left2, right2, corners,
     in_sem, send1, recv1, send2, recv2,
 ):
     n_x, n_y = sizes
@@ -108,7 +108,8 @@
         fetch.start()
 
     own = pl.ds(HALO, rx)
-    zeros = jnp.zeros((2 * nz + 1, HALO, ry), f32)
+    planes = nz + 1 + nz // 2
+    zeros = jnp.zeros((planes, HALO, ry), f32)
     ext[:, pl.ds(0, HALO), :] = zeros
     ext[:, pl.ds(HALO + rx, HALO), :] = zeros
     for ref in (from_left, from_right, up, down, left2, right2, corners):
@@ -128,8 +129,13 @@
         fetch.wait()
     for z in range(nz):
         ext[z, own, :] = state[z]
-        ext[nz + z, own, :] = load[z].astype(f32)
-    ext[2 * nz, own, :] = active[...].astype(f32)
+        lf[z, own, :] = load[z].astype(f32)
+    ext[nz, own, :] = active[...].astype(f32)
+    top = iota((HALO, ry), 0) < QUARTER
+    for j in range(nz // 2):
+        for r, natural in ((HALO, top), (rx, ~top)):
+            odd = pltpu.roll(lf[2 * j + 1, pl.ds(r, HALO), :], QUARTER, 0)
+            ext[nz + 1 + j, pl.ds(r, HALO), :] = jnp.where(natural, lf[2 * j, pl.ds(r, HALO), :], odd)
 
     lane = iota((rx, LANES), 1)
     group = (lane & (half - 1)) >> 3
@@ -137,10 +143,10 @@
     lows = (lane & (HALF - 1)) < QUARTER
     to_right = jnp.zeros((rx, LANES), f32)
     to_left = jnp.zeros((rx, LANES), f32)
-    act = ext[2 * nz, own, :]
+    act = ext[nz, own, :]
     for z in range(nz):
         s = ext[z, own, :]
-        l = pltpu.roll(ext[nz + z, own, :], (half + QUARTER + HALF * z) % LANES, 1)
+        l = pltpu.roll(lf[z, own, :], (half + QUARTER + HALF * z) % LANES, 1)
         mine = group == z
         first = mine & high & lows
         second = mine & high & ~lows
@@ -174,7 +180,7 @@
     def copy2(i):
         dx, dy = DIRS[i]
         if dy == 0:
-            src = tot.at[:, pl.ds(HALO + rx if dx > 0 else 0, HALO), :]
+            src = rim_x.at[0 if dx > 0 else 1]
             dst = up if dx > 0 else down
         elif dx == 0:
             src = edge.at[pl.ds(HALO, rx), :]
@@ -213,8 +219,8 @@
     distance = jnp.abs(outer_y(iota((full, 1), 0), ry) - inner_y(iota((1, full), 1), ry))
     for j, taps in enumerate((mass, stiff)):
         h, l = split(band_of(distance, [taps[2, k] for k in range(BAND + 1)]))
-        yb_hi[:, pl.ds(j * full, full)] = h
-        yb_lo[:, pl.ds(j * full, full)] = l
+        for i, part in enumerate((h, h, l)):
+            yb[pl.ds(i * full, full), pl.ds(j * full, full)] = part
 
     highest = lax.Precision.HIGHEST
     tile_y = jnp.dot(
@@ -226,8 +232,9 @@
     for t in range(PATCH):
         wy = jnp.where(place == t, tile_y[t : t + 1, :], wy)
     h, l = split(wy)
-    wy_hi[...] = h
-    wy_lo[...] = l
+    for i, part in enumerate((h, h, l)):
+        wy3[pl.ds(i * full, full), :] = part
+        wyt3[:, pl.ds(i * qy, qy)] = part
 
     def wx_of(shape, reps_r, reps_c):
         r, c = iota((shape[0], 1), 0), iota((1, shape[1]), 1)
@@ -267,7 +274,9 @@
     y_in = inner_y(iota((full, 1), 0), ry)
     y_to = iota((1, cells), 1) & (PATCH - 1)
     for m in range(slots):
-        sel[m] = jnp.where(y_in + QUARTER - HALF * cut_b[m] == y_to, 1.0, 0.0).astype(bf16)
+        one_hot = jnp.where(y_in + QUARTER - HALF * cut_b[m] == y_to, 1.0, 0.0).astype(bf16)
+        sel[m, pl.ds(0, full), :] = one_hot
+        sel[m, pl.ds(full, full), :] = one_hot
 
     def pick(shape, dim, row):
         index = iota(shape, dim) & (PATCH - 1)
@@ -295,6 +304,11 @@
         for z in range(nz):
             v = jnp.where((group1 == z) & (lane1 >= half), basis_s[0, QUARTER + z, k], v)
         v_vec.append(v)
+
+    def put3(ref, rows, start, width, v):
+        h, l = split(v)
+        for i, part in enumerate((h, l, h)):
+            ref[rows, pl.ds(i * width + start, v.shape[1])] = part
 
     def mix_z(start, count):
         for r in range(start, start + count, HALF):
@@ -313,6 +327,7 @@
                 zm[z, rows, :] = q
 
     mix_z(HALO, rx)
+    fetches[9].wait()
     wait_recv_all(copy1)
     mix_z(0, HALO)
     mix_z(HALO + rx, HALO)
@@ -325,22 +340,19 @@
     load_t = jnp.where(low, halo_l, halo_r)
     act_t = jnp.where(low, pltpu.roll(halo_l, LANES - QUARTER, 1), pltpu.roll(halo_r, QUARTER, 1))
     act_t = jnp.where(lane_w >= half, act_t, 0.0)
-    act_w = ext[2 * nz]
+    act_w = ext[nz]
+    for z in range(nz):
+        for r in (0, HALO + rx):
+            tile = ext[nz + 1 + z // 2, pl.ds(r, HALO), :]
+            lf[z, pl.ds(r, HALO), :] = pltpu.roll(tile, QUARTER, 0) if z % 2 else tile
     for z in range(nz):
         rows = pl.ds(z * wide, wide)
-        for hi, lo, mixed, vec in ((sk_hi, sk_lo, zk, k_vec), (sm_hi, sm_lo, zm, m_vec)):
-            h, l = split(mixed[z])
-            hi[rows, pl.ds(0, ry)] = h
-            lo[rows, pl.ds(0, ry)] = l
-            h, l = split(comb * vec[z])
-            hi[rows, pl.ds(ry, LANES)] = h
-            lo[rows, pl.ds(ry, LANES)] = l
-
-    def times(hi, lo, w_hi, w_lo):
-        return dot(hi, w_hi) + dot(lo, w_hi) + dot(hi, w_lo)
-
-    ym = times(sm_hi[...], sm_lo[...], yb_hi[...], yb_lo[...])
-    yp = ym[:, full:] + times(sk_hi[...], sk_lo[...], yb_hi[:, pl.ds(0, full)], yb_lo[:, pl.ds(0, full)])
+        for s3, mixed, vec in ((sk3, zk, k_vec), (sm3, zm, m_vec)):
+            put3(s3, rows, 0, full, mixed[z])
+            put3(s3, rows, ry, full, comb * vec[z])
+
+    ym = dot(sm3[...], yb[...])
+    yp = ym[:, full:] + dot(sk3[...], yb[:, pl.ds(0, full)])
 
     r0 = []
     r1 = jnp.zeros((wide, LANES), f32)
@@ -349,7 +361,7 @@
         q_hi, q_lo = split(ym[z * wide : (z + 1) * wide, :full])
         applied = dot(bx_hi, jnp.concatenate([p_hi, q_hi, p_lo, q_lo], axis=0))
         applied = applied + dot(bx_lo, jnp.concatenate([p_hi, q_hi], axis=0))
-        r0.append(act_w * (ext[nz + z] - applied[:, :ry]))
+        r0.append(act_w * (lf[z] - applied[:, :ry]))
         r1 = jnp.where(group_w == z, applied[:, ry:], r1)
     r1 = act_t * (load_t - r1)
 
@@ -359,21 +371,16 @@
         for z in range(nz):
             term = basis_s[0, QUARTER + z, k] * r0[z]
             v = term if v is None else v + term
-        h, l = split(v)
-        r_hi[rows, pl.ds(0, ry)] = h
-        r_lo[rows, pl.ds(0, ry)] = l
-        h, l = split(r1 * v_vec[k])
-        r_hi[rows, pl.ds(ry, LANES)] = h
-        r_lo[rows, pl.ds(ry, LANES)] = l
-
-    fetches[9].wait()
+        put3(r3, rows, 0, full, v)
+        put3(r3, rows, ry, full, r1 * v_vec[k])
+
     vz = basis[0, pl.ds(QUARTER, nz), :]
     cell_x = iota((1, cells), 1) >> 4
     row_k = iota((PATCH, cells), 0)
     spread = []
     for m in range(slots):
         spot = (iota((wide, 1), 0) - (HALO - QUARTER) - HALF * cut_a[m]) == cell_x
-        taken = (dot(r_hi[...], sel[m]) + dot(r_lo[...], sel[m])).reshape(PATCH, wide, cells)
+        taken = dot(r3[:, pl.ds(0, 2 * full)], sel[m]).reshape(PATCH, wide, cells)
         zmodes = jnp.sum(jnp.where(spot[None], taken, 0.0), axis=1).astype(bf16)
         dense = jnp.zeros((PATCH, cells), f32)
         for k in range(PATCH):
@@ -382,23 +389,19 @@
         corr = jnp.where(cut[m] >= 0, corr, 0.0)
         spread.append(jnp.where(spot[None], corr[:, None, :], 0.0).reshape(nz * wide, cells))
 
-    t1 = times(r_hi[...], r_lo[...], wy_hi[...], wy_lo[...])
+    t1 = dot(r3[...], wy3[...])
     for k in range(PATCH):
         h, l = split(t1[k * wide : (k + 1) * wide])
         u = (dot(g_hi, jnp.concatenate([h, l], axis=0)) + dot(g_lo, h)) * dinv[k]
         h, l = split(u)
         back = dot(b_hi, jnp.concatenate([h, l], axis=0)) + dot(b_lo, h)
-        h, l = split(back)
-        tb_hi[pl.ds(k * wide, wide), :] = h
-        tb_lo[pl.ds(k * wide, wide), :] = l
-    fast = (
-        dot_nt(tb_hi[...], wy_hi[...]) + dot_nt(tb_lo[...], wy_hi[...]) + dot_nt(tb_hi[...], wy_lo[...])
-    ).reshape(PATCH, wide, full)
+        put3(tb3, pl.ds(k * wide, wide), 0, qy, back)
+    fast = dot_nt(tb3[...], wyt3[...]).reshape(PATCH, wide, full)
 
     cut_total = None
     for m in range(slots):
         h, l = split(spread[m])
-        term = dot_nt(h, sel[m]) + dot_nt(l, sel[m])
+        term = dot_nt(h, sel[m, pl.ds(0, full), :]) + dot_nt(l, sel[m, pl.ds(0, full), :])
         cut_total = term if cut_total is None else cut_total + term
     cut_total = cut_total.reshape(nz, wide, full)
 
@@ -413,8 +416,13 @@
         for k in range(PATCH):
             t = t + basis_s[0, QUARTER + z, k] * fast[k, :, :ry]
         tot[z] = t
+    for j in range(nz // 2):
+        for i, r, natural in ((0, HALO + rx, top), (1, 0, ~top)):
+            odd = pltpu.roll(tot[2 * j + 1, pl.ds(r, HALO), :], QUARTER, 0)
+            rim_x[i, j] = jnp.where(natural, tot[2 * j, pl.ds(r, HALO), :], odd)
 
     start_all(copy2)
+    wait_send_all(copy1)
     wait_recv_all(copy2)
 
     gap = jnp.zeros((rx - 2 * HALO, LANES), f32)
@@ -422,14 +430,16 @@
     r2 = right2[...] + jnp.concatenate([corners[1], gap, corners[3]], axis=0)
     both = jnp.where(lows, r2, l2)
     rim = (lane < QUARTER) | (lane >= ry - QUARTER)
-    scale = damping * ext[2 * nz, own, :]
+    scale = damping * ext[nz, own, :]
     for z in range(nz):
         moved = pltpu.roll(both, (LANES - QUARTER - half - HALF * z) % LANES, 1)
-        t = tot[z, own, :] + jnp.concatenate([up[z], gap, down[z]], axis=0)
+        u, d = up[z // 2], down[z // 2]
+        if z % 2:
+            u, d = pltpu.roll(u, QUARTER, 0), pltpu.roll(d, QUARTER, 0)
+        t = tot[z, own, :] + jnp.concatenate([jnp.where(top, u, 0.0), gap, jnp.where(top, 0.0, d)], axis=0)
         t = t + jnp.where(rim, moved, 0.0)
         out[z] = state[z] + scale * t
 
-    wait_send_all(copy1)
     wait_send_all(copy2)
 
 
@@ -444,13 +454,13 @@
     full = ry + LANES
     qx, qy = (rx // HALF) * PATCH, (ry // HALF) * PATCH
     cells = PATCH * PATCH
-    anyspace = pl.BlockSpec(memory_space=pl.ANY)
+    anyspace = pl.BlockSpec(memory_space=pltpu.HBM)
     V, S = pltpu.VMEM, pltpu.SMEM
     dma = pltpu.SemaphoreType.DMA
     n = len(DIRS)
     return pl.pallas_call(
         functools.partial(kernel, sizes),
-        out_shape=jax.ShapeDtypeStruct(state.shape, f32),
+        out_shape=pltpu.VMEM(state.shape, f32),
         in_specs=[anyspace] * 9,
         out_specs=pl.BlockSpec(memory_space=pltpu.VMEM),
         scratch_shapes=[
@@ -458,20 +468,18 @@
             S(stiff_band.shape, f32), S(mass_band.shape, f32), S(eig_basis.shape, f32),
             V(eig_basis.shape, f32), S(eig_values.shape, f32), S(cut_cols.shape, cut_cols.dtype),
             V((slots, PATCH, cells, cells), bf16),
-            V((2 * nz + 1, wide, ry), f32),
+            V((nz + 1 + nz // 2, wide, ry), f32), V((nz, wide, ry), f32),
             V((wide, LANES), f32), V((wide, LANES), f32),
             V((rx, LANES), f32), V((rx, LANES), f32),
-            V((full, 2 * full), bf16), V((full, 2 * full), bf16),
-            V((full, qy), bf16), V((full, qy), bf16),
-            V((slots, full, cells), bf16),
+            V((3 * full, 2 * full), bf16), V((3 * full, qy), bf16), V((full, 3 * qy), bf16),
+            V((slots, 2 * full, cells), bf16),
             V((PATCH, qx, qy), f32),
             V((nz, wide, ry), f32), V((nz, wide, ry), f32),
-            V((nz * wide, full), bf16), V((nz * wide, full), bf16),
-            V((nz * wide, full), bf16), V((nz * wide, full), bf16),
-            V((PATCH * wide, full), bf16), V((PATCH * wide, full), bf16),
-            V((PATCH * wide, qy), bf16), V((PATCH * wide, qy), bf16),
+            V((nz * wide, 3 * full), bf16), V((nz * wide, 3 * full), bf16),
+            V((PATCH * wide, 3 * full), bf16), V((PATCH * wide, 3 * qy), bf16),
             V((nz, wide, ry), f32), V((wide, LANES), f32),
-            V((nz, HALO, ry), f32), V((nz, HALO, ry), f32),
+            V((2, nz // 2, HALO, ry), f32),
+            V((nz // 2, HALO, ry), f32), V((nz // 2, HALO, ry), f32),
             V((rx, LANES), f32), V((rx, LANES), f32),
             V((4, HALO, LANES), f32),
             dma((10,)), dma((n,)), dma((n,)), dma((n,)), dma((n,)),

time: 22 us -> 19.7 us (0.90)
  Pallas kernels: 20.3 us -> 18.9 us
  local copies, waits for them, and re-layouts: 1.57 us -> 0.66 us
    pallas_call x1, Pallas kernels: 20.3 us -> 18.9 us  [on_device(): pl.pallas_call(functools.partial(kernel, sizes), out_shape=pltpu.VMEM(sta...]
    unnamed x1, local copies, waits for them, and re-layouts: 1.57 us -> 0.66 us
where the time goes in v3:
time: 19.7 us; the launch traced here: 19.5 us
  Pallas kernels  18.9 us (96%)
  local copies, waits for them, and re-layouts  0.66 us (3%)
    pallas_call x1, Pallas kernels, on_device(): pl.pallas_call(functools.partial(kernel, sizes), out_shape=pltpu.VMEM(sta...  18.9 us
    unnamed x1, local copies, waits for them, and re-layouts  0.66 us

profile of v3, /device:TPU:13, one launch (start us, length us, event | category | flops | bytes accessed | tf_op | source)
XLA Modules:
  0.0 19.5 jit_solution(16626528907903144317)
XLA Ops:
  0.0 18.9 %shard_map.91 = f32[8,32,128]{2,1,0:T(8,128)S(1)} custom-call(f32[8,32,128]{2,1,0:T(8,128)} %state_h.1, bf16[8,32,128]{2,1,0:T(8,128)(2,1)} %load_h.1, s32[32,128]{1,0:T(8,128)} %active_h.1, f32[3,5]{1,0:T(4,128)} %stiff_h.1, f32[3,5]{1,0:T(4,128)} %mass_h.1, f32[3,16,16]{2,1,0:T(8,128)} %basis_h.1, f32[3,16]{1,0:T(4,128)} %values_h.1, s32[1,1,2]{2,1,0:T(1,128)} %cols_h.1, ...), custom_call_target="tpu_custom_call" | custom-call | tf_op jit(solution)/shard_map/pallas_call | solution.py:461
  18.9 0.7 %copy.11 = f32[8,32,128]{2,1,0:T(8,128)} copy(f32[8,32,128]{2,1,0:T(8,128)S(1)} %shard_map.91) | data formatting | bytes 262144

commit v4 on v3

--- a/solution.py
+++ b/solution.py
@@ -69,7 +69,7 @@
     out,
     state, load, active, stiff, mass, basis_s, basis, values, cols, inv,
     ext, lf, from_left, from_right, pack_left, pack_right,
-    yb, wy3, wyt3, sel, dinv,
+    yb, wy3, wyt3, sel, sel_t, dinv, rs, cw,
     zk, zm, sk3, sm3, r3, tb3, tot, edge,
     rim_x, up, down, left2, right2, corners,
     in_sem, send1, recv1, send2, recv2,
@@ -234,7 +234,10 @@
     h, l = split(wy)
     for i, part in enumerate((h, h, l)):
         wy3[pl.ds(i * full, full), :] = part
-        wyt3[:, pl.ds(i * qy, qy)] = part
+
+    h, l = split(wy.T)
+    for i, part in enumerate((h, h, l)):
+        wyt3[pl.ds(i * qy, qy), :] = part
 
     def wx_of(shape, reps_r, reps_c):
         r, c = iota((shape[0], 1), 0), iota((1, shape[1]), 1)
@@ -249,13 +252,14 @@
             w = jnp.where(t == k, tile[k : k + 1, :], w)
         return w
 
-    pad_r = -(-2 * wide // LANES) * LANES
+    def split3(v, width):
+        h, l = split(v)
+        return jnp.where(iota((1, v.shape[1]), 1) < 2 * width, h.astype(f32), l.astype(f32)).astype(bf16)
+
+    pad_r = -(-3 * wide // LANES) * LANES
     pad_c = -(-qx // LANES) * LANES
-    gx2 = wx_of((pad_r, pad_c), 2, 1).T[:qx, : 2 * wide]
-    g_hi, g_lo = split(gx2)
-    g_lo = g_lo[:, :wide]
-    b_hi, b_lo = split(wx_of((wide, 2 * qx), 1, 2))
-    b_lo = b_lo[:, :qx]
+    g3 = split3(wx_of((pad_r, pad_c), 3, 1).T[:qx, : 3 * wide], wide)
+    b3 = split3(wx_of((wide, 3 * qx), 1, 3), qx)
 
     c = iota((1, 4 * wide), 1)
     dist_x = jnp.abs(iota((wide, 1), 0) - wrap(c, wide, 4))
@@ -273,10 +277,20 @@
     cut_b = [lax.rem(jnp.maximum(v, 0), jnp.int32(blocks_y)) for v in cut]
     y_in = inner_y(iota((full, 1), 0), ry)
     y_to = iota((1, cells), 1) & (PATCH - 1)
+    y_in_t = inner_y(iota((1, full), 1), ry)
+    y_to_t = iota((cells, 1), 0) & (PATCH - 1)
     for m in range(slots):
-        one_hot = jnp.where(y_in + QUARTER - HALF * cut_b[m] == y_to, 1.0, 0.0).astype(bf16)
-        sel[m, pl.ds(0, full), :] = one_hot
-        sel[m, pl.ds(full, full), :] = one_hot
+        sel[m] = jnp.where(y_in + QUARTER - HALF * cut_b[m] == y_to, 1.0, 0.0).astype(bf16)
+        sel_t[m] = jnp.where(y_in_t + QUARTER - HALF * cut_b[m] == y_to_t, 1.0, 0.0).astype(bf16)
+
+    near = PATCH + HALF
+    spot = iota((near, 1), 0) - QUARTER == (iota((1, cells), 1) >> 4)
+    vz_t = []
+    for z in range(nz):
+        v = jnp.zeros((PATCH, 1), f32)
+        for k in range(PATCH):
+            v = jnp.where(iota((PATCH, 1), 0) == k, basis_s[0, QUARTER + z, k], v)
+        vz_t.append(v)
 
     def pick(shape, dim, row):
         index = iota(shape, dim) & (PATCH - 1)
@@ -374,54 +388,72 @@
         put3(r3, rows, 0, full, v)
         put3(r3, rows, ry, full, r1 * v_vec[k])
 
+    for z in range(nz):
+        rs[z, :, pl.ds(0, ry)] = r0[z]
+        rs[z, :, pl.ds(ry, LANES)] = jnp.where(group_w == z, r1, 0.0)
     vz = basis[0, pl.ds(QUARTER, nz), :]
-    cell_x = iota((1, cells), 1) >> 4
-    row_k = iota((PATCH, cells), 0)
-    spread = []
     for m in range(slots):
-        spot = (iota((wide, 1), 0) - (HALO - QUARTER) - HALF * cut_a[m]) == cell_x
-        taken = dot(r3[:, pl.ds(0, 2 * full)], sel[m]).reshape(PATCH, wide, cells)
-        zmodes = jnp.sum(jnp.where(spot[None], taken, 0.0), axis=1).astype(bf16)
-        dense = jnp.zeros((PATCH, cells), f32)
+        window = rs[:, pl.ds(0, near), :]
+        for a in range(1, blocks_x):
+            window = jnp.where(cut_a[m] == a, rs[:, pl.ds(a * HALF, near), :], window)
+        h, l = split(window.reshape(nz * near, full))
+        taken = (dot(h, sel[m]) + dot(l, sel[m])).reshape(nz, near, cells)
+        patch = jnp.sum(jnp.where(spot[None], taken, 0.0), axis=1)
+        zmodes = None
+        for z in range(nz):
+            term = vz_t[z] * patch[z : z + 1, :]
+            zmodes = term if zmodes is None else zmodes + term
+        zmodes = zmodes.astype(bf16)
+        corr = jnp.zeros((nz, cells), f32)
         for k in range(PATCH):
-            dense = jnp.where(row_k == k, dot_nt(zmodes, inv[m, k]), dense)
-        corr = jnp.dot(vz, dense, precision=highest, preferred_element_type=f32)
+            corr = corr + vz[:, k : k + 1] * dot_nt(zmodes, inv[m, k])[k : k + 1, :]
         corr = jnp.where(cut[m] >= 0, corr, 0.0)
-        spread.append(jnp.where(spot[None], corr[:, None, :], 0.0).reshape(nz * wide, cells))
+        h, l = split(jnp.where(spot[None], corr[:, None, :], 0.0).reshape(nz * near, cells))
+        placed = (dot(h, sel_t[m]) + dot(l, sel_t[m])).reshape(nz, near, full)
+        cw[m] = placed
 
     t1 = dot(r3[...], wy3[...])
     for k in range(PATCH):
         h, l = split(t1[k * wide : (k + 1) * wide])
-        u = (dot(g_hi, jnp.concatenate([h, l], axis=0)) + dot(g_lo, h)) * dinv[k]
-        h, l = split(u)
-        back = dot(b_hi, jnp.concatenate([h, l], axis=0)) + dot(b_lo, h)
+        h, l = split(dot(g3, jnp.concatenate([h, l, h], axis=0)) * dinv[k])
+        back = dot(b3, jnp.concatenate([h, l, h], axis=0))
         put3(tb3, pl.ds(k * wide, wide), 0, qy, back)
-    fast = dot_nt(tb3[...], wyt3[...]).reshape(PATCH, wide, full)
-
-    cut_total = None
-    for m in range(slots):
-        h, l = split(spread[m])
-        term = dot_nt(h, sel[m, pl.ds(0, full), :]) + dot_nt(l, sel[m, pl.ds(0, full), :])
-        cut_total = term if cut_total is None else cut_total + term
-    cut_total = cut_total.reshape(nz, wide, full)
+    fast = dot(tb3[...], wyt3[...]).reshape(PATCH, wide, full)
+
+    def cut_part(z, start, count, lanes):
+        tiles = []
+        for r in range(start // HALF, (start + count) // HALF):
+            out = jnp.zeros((HALF, LANES), f32)
+            for m in range(slots):
+                for a in range(blocks_x):
+                    if 0 <= r - a < near // HALF:
+                        out = out + jnp.where(cut_a[m] == a, cw[m, z, pl.ds((r - a) * HALF, HALF), lanes], 0.0)
+            tiles.append(out)
+        return jnp.concatenate(tiles, axis=0)
+
+    def total_rows(z, start, count):
+        t = cut_part(z, start, count, pl.ds(0, ry))
+        for k in range(PATCH):
+            t = t + basis_s[0, QUARTER + z, k] * fast[k, start : start + count, :ry]
+        tot[z, pl.ds(start, count), :] = t
 
     packed = jnp.zeros((wide, LANES), f32)
     for z in range(nz):
-        packed = jnp.where(group_w == z, cut_total[z, :, ry:], packed)
+        packed = jnp.where(group_w == z, cut_part(z, 0, wide, pl.ds(ry, LANES)), packed)
     for k in range(PATCH):
         packed = packed + v_vec[k] * fast[k, :, ry:]
     edge[...] = packed
     for z in range(nz):
-        t = cut_total[z, :, :ry]
-        for k in range(PATCH):
-            t = t + basis_s[0, QUARTER + z, k] * fast[k, :, :ry]
-        tot[z] = t
+        total_rows(z, 0, HALO)
+        total_rows(z, HALO + rx, HALO)
     for j in range(nz // 2):
         for i, r, natural in ((0, HALO + rx, top), (1, 0, ~top)):
             odd = pltpu.roll(tot[2 * j + 1, pl.ds(r, HALO), :], QUARTER, 0)
             rim_x[i, j] = jnp.where(natural, tot[2 * j, pl.ds(r, HALO), :], odd)
 
     start_all(copy2)
+    for z in range(nz):
+        total_rows(z, HALO, rx)
     wait_send_all(copy1)
     wait_recv_all(copy2)
 
@@ -471,9 +503,10 @@
             V((nz + 1 + nz // 2, wide, ry), f32), V((nz, wide, ry), f32),
             V((wide, LANES), f32), V((wide, LANES), f32),
             V((rx, LANES), f32), V((rx, LANES), f32),
-            V((3 * full, 2 * full), bf16), V((3 * full, qy), bf16), V((full, 3 * qy), bf16),
-            V((slots, 2 * full, cells), bf16),
+            V((3 * full, 2 * full), bf16), V((3 * full, qy), bf16), V((3 * qy, full), bf16),
+            V((slots, full, cells), bf16), V((slots, cells, full), bf16),
             V((PATCH, qx, qy), f32),
+            V((nz, wide, full), f32), V((slots, nz, PATCH + HALF, full), f32),
             V((nz, wide, ry), f32), V((nz, wide, ry), f32),
             V((nz * wide, 3 * full), bf16), V((nz * wide, 3 * full), bf16),
             V((PATCH * wide, 3 * full), bf16), V((PATCH * wide, 3 * qy), bf16),

time: 19.7 us -> 18.1 us (0.919)
  Pallas kernels: 18.9 us -> 17.3 us
    pallas_call x1, Pallas kernels: 18.9 us -> 17.3 us  [on_device(): pl.pallas_call(functools.partial(kernel, sizes), out_shape=pltpu.VMEM(sta...]
where the time goes in v4:
time: 18.1 us; the launch traced here: 17.9 us
  Pallas kernels  17.3 us (96%)
  local copies, waits for them, and re-layouts  0.66 us (4%)
    pallas_call x1, Pallas kernels, on_device(): pl.pallas_call(functools.partial(kernel, sizes), out_shape=pltpu.VMEM(sta...  17.3 us
    unnamed x1, local copies, waits for them, and re-layouts  0.66 us

profile of v4, /device:TPU:13, one launch (start us, length us, event | category | flops | bytes accessed | tf_op | source)
XLA Modules:
  0.0 17.9 jit_solution(5858813623298553205)
XLA Ops:
  0.0 17.3 %shard_map.91 = f32[8,32,128]{2,1,0:T(8,128)S(1)} custom-call(f32[8,32,128]{2,1,0:T(8,128)} %state_h.1, bf16[8,32,128]{2,1,0:T(8,128)(2,1)} %load_h.1, s32[32,128]{1,0:T(8,128)} %active_h.1, f32[3,5]{1,0:T(4,128)} %stiff_h.1, f32[3,5]{1,0:T(4,128)} %mass_h.1, f32[3,16,16]{2,1,0:T(8,128)} %basis_h.1, f32[3,16]{1,0:T(4,128)} %values_h.1, s32[1,1,2]{2,1,0:T(1,128)} %cols_h.1, ...), custom_call_target="tpu_custom_call" | custom-call | tf_op jit(solution)/shard_map/pallas_call | solution.py:493
  17.3 0.7 %copy.11 = f32[8,32,128]{2,1,0:T(8,128)} copy(f32[8,32,128]{2,1,0:T(8,128)S(1)} %shard_map.91) | data formatting | bytes 262144

commit v5 on v4

--- a/solution.py
+++ b/solution.py
@@ -32,10 +32,6 @@
 
 def dot(a, b):
     return jnp.dot(a, b, preferred_element_type=f32)
-
-
-def dot_nt(a, b):
-    return lax.dot_general(a, b, (((1,), (1,)), ((), ())), preferred_element_type=f32)
 
 
 def band_of(distance, taps):
@@ -403,10 +399,13 @@
         for z in range(nz):
             term = vz_t[z] * patch[z : z + 1, :]
             zmodes = term if zmodes is None else zmodes + term
-        zmodes = zmodes.astype(bf16)
-        corr = jnp.zeros((nz, cells), f32)
+        zmodes = zmodes.T.astype(bf16)
+        dense = jnp.zeros((cells, PATCH), f32)
         for k in range(PATCH):
-            corr = corr + vz[:, k : k + 1] * dot_nt(zmodes, inv[m, k])[k : k + 1, :]
+            dense = jnp.where(iota((1, PATCH), 1) == k, dot(inv[m, k], zmodes), dense)
+        corr = lax.dot_general(
+            vz, dense, (((1,), (1,)), ((), ())), precision=highest, preferred_element_type=f32
+        )
         corr = jnp.where(cut[m] >= 0, corr, 0.0)
         h, l = split(jnp.where(spot[None], corr[:, None, :], 0.0).reshape(nz * near, cells))
         placed = (dot(h, sel_t[m]) + dot(l, sel_t[m])).reshape(nz, near, full)

time: 18.1 us -> 19.5 us (1.077)
  Pallas kernels: 17.3 us -> 18.6 us
    pallas_call x1, Pallas kernels: 17.3 us -> 18.6 us  [on_device(): pl.pallas_call(functools.partial(kernel, sizes), out_shape=pltpu.VMEM(sta...]
where the time goes in v5:
time: 19.5 us; the launch traced here: 19.3 us
  Pallas kernels  18.6 us (95%)
  local copies, waits for them, and re-layouts  0.66 us (3%)
    pallas_call x1, Pallas kernels, on_device(): pl.pallas_call(functools.partial(kernel, sizes), out_shape=pltpu.VMEM(sta...  18.6 us
    unnamed x1, local copies, waits for them, and re-layouts  0.66 us

profile of v5, /device:TPU:13, one launch (start us, length us, event | category | flops | bytes accessed | tf_op | source)
XLA Modules:
  0.0 19.3 jit_solution(9110483742281894168)
XLA Ops:
  0.0 18.6 %shard_map.91 = f32[8,32,128]{2,1,0:T(8,128)S(1)} custom-call(f32[8,32,128]{2,1,0:T(8,128)} %state_h.1, bf16[8,32,128]{2,1,0:T(8,128)(2,1)} %load_h.1, s32[32,128]{1,0:T(8,128)} %active_h.1, f32[3,5]{1,0:T(4,128)} %stiff_h.1, f32[3,5]{1,0:T(4,128)} %mass_h.1, f32[3,16,16]{2,1,0:T(8,128)} %basis_h.1, f32[3,16]{1,0:T(4,128)} %values_h.1, s32[1,1,2]{2,1,0:T(1,128)} %cols_h.1, ...), custom_call_target="tpu_custom_call" | custom-call | tf_op jit(solution)/shard_map/pallas_call | solution.py:492
  18.6 0.7 %copy.11 = f32[8,32,128]{2,1,0:T(8,128)} copy(f32[8,32,128]{2,1,0:T(8,128)S(1)} %shard_map.91) | data formatting | bytes 262144

commit v6 on v4

--- a/solution.py
+++ b/solution.py
@@ -359,66 +359,122 @@
         for r in (0, HALO + rx):
             tile = ext[nz + 1 + z // 2, pl.ds(r, HALO), :]
             lf[z, pl.ds(r, HALO), :] = pltpu.roll(tile, QUARTER, 0) if z % 2 else tile
-    for z in range(nz):
-        rows = pl.ds(z * wide, wide)
-        for s3, mixed, vec in ((sk3, zk, k_vec), (sm3, zm, m_vec)):
-            put3(s3, rows, 0, full, mixed[z])
-            put3(s3, rows, ry, full, comb * vec[z])
-
-    ym = dot(sm3[...], yb[...])
-    yp = ym[:, full:] + dot(sk3[...], yb[:, pl.ds(0, full)])
-
     r0 = []
     r1 = jnp.zeros((wide, LANES), f32)
-    for z in range(nz):
-        p_hi, p_lo = split(yp[z * wide : (z + 1) * wide])
-        q_hi, q_lo = split(ym[z * wide : (z + 1) * wide, :full])
-        applied = dot(bx_hi, jnp.concatenate([p_hi, q_hi, p_lo, q_lo], axis=0))
-        applied = applied + dot(bx_lo, jnp.concatenate([p_hi, q_hi], axis=0))
-        r0.append(act_w * (lf[z] - applied[:, :ry]))
-        r1 = jnp.where(group_w == z, applied[:, ry:], r1)
+    part_z = nz // 2
+
+    def spread_y(g):
+        for z in range(g * part_z, (g + 1) * part_z):
+            rows = pl.ds(z * wide, wide)
+            for s3, mixed, vec in ((sk3, zk, k_vec), (sm3, zm, m_vec)):
+                put3(s3, rows, 0, full, mixed[z])
+                put3(s3, rows, ry, full, comb * vec[z])
+
+    def band_y(g):
+        rows = pl.ds(g * part_z * wide, part_z * wide)
+        ym = dot(sm3[rows, :], yb[...])
+        return ym[:, :full], ym[:, full:] + dot(sk3[rows, :], yb[:, pl.ds(0, full)])
+
+    def band_x(g, ym, yp, r1):
+        for i in range(part_z):
+            z = g * part_z + i
+            p_hi, p_lo = split(yp[i * wide : (i + 1) * wide])
+            q_hi, q_lo = split(ym[i * wide : (i + 1) * wide])
+            applied = dot(bx_hi, jnp.concatenate([p_hi, q_hi, p_lo, q_lo], axis=0))
+            applied = applied + dot(bx_lo, jnp.concatenate([p_hi, q_hi], axis=0))
+            r0.append(act_w * (lf[z] - applied[:, :ry]))
+            r1 = jnp.where(group_w == z, applied[:, ry:], r1)
+        return r1
+
+    spread_y(0)
+    first_half = band_y(0)
+    spread_y(1)
+    second_half = band_y(1)
+    r1 = band_x(0, *first_half, r1)
+    r1 = band_x(1, *second_half, r1)
     r1 = act_t * (load_t - r1)
 
-    for k in range(PATCH):
-        rows = pl.ds(k * wide, wide)
-        v = None
-        for z in range(nz):
-            term = basis_s[0, QUARTER + z, k] * r0[z]
-            v = term if v is None else v + term
-        put3(r3, rows, 0, full, v)
-        put3(r3, rows, ry, full, r1 * v_vec[k])
-
-    for z in range(nz):
-        rs[z, :, pl.ds(0, ry)] = r0[z]
-        rs[z, :, pl.ds(ry, LANES)] = jnp.where(group_w == z, r1, 0.0)
+    per = PATCH // 4
     vz = basis[0, pl.ds(QUARTER, nz), :]
-    for m in range(slots):
+    t1, fast = {}, {}
+    zmodes, corr = {}, {}
+
+    def to_modes(g):
+        for k in range(g * per, (g + 1) * per):
+            rows = pl.ds(k * wide, wide)
+            v = None
+            for z in range(nz):
+                term = basis_s[0, QUARTER + z, k] * r0[z]
+                v = term if v is None else v + term
+            put3(r3, rows, 0, full, v)
+            put3(r3, rows, ry, full, r1 * v_vec[k])
+
+    def to_y(g):
+        t1[g] = dot(r3[pl.ds(g * per * wide, per * wide), :], wy3[...])
+
+    def solve_x(g):
+        for i in range(per):
+            k = g * per + i
+            h, l = split(t1[g][i * wide : (i + 1) * wide])
+            h, l = split(dot(g3, jnp.concatenate([h, l, h], axis=0)) * dinv[k])
+            back = dot(b3, jnp.concatenate([h, l, h], axis=0))
+            put3(tb3, pl.ds(k * wide, wide), 0, qy, back)
+
+    def from_y(g):
+        fast[g] = dot(tb3[pl.ds(g * per * wide, per * wide), :], wyt3[...])
+
+    def cut_take(m):
         window = rs[:, pl.ds(0, near), :]
         for a in range(1, blocks_x):
             window = jnp.where(cut_a[m] == a, rs[:, pl.ds(a * HALF, near), :], window)
         h, l = split(window.reshape(nz * near, full))
         taken = (dot(h, sel[m]) + dot(l, sel[m])).reshape(nz, near, cells)
         patch = jnp.sum(jnp.where(spot[None], taken, 0.0), axis=1)
-        zmodes = None
+        modes = None
         for z in range(nz):
             term = vz_t[z] * patch[z : z + 1, :]
-            zmodes = term if zmodes is None else zmodes + term
-        zmodes = zmodes.astype(bf16)
-        corr = jnp.zeros((nz, cells), f32)
+            modes = term if modes is None else modes + term
+        zmodes[m] = modes.astype(bf16)
+
+    def cut_solve(m):
+        c = jnp.zeros((nz, cells), f32)
         for k in range(PATCH):
-            corr = corr + vz[:, k : k + 1] * dot_nt(zmodes, inv[m, k])[k : k + 1, :]
-        corr = jnp.where(cut[m] >= 0, corr, 0.0)
-        h, l = split(jnp.where(spot[None], corr[:, None, :], 0.0).reshape(nz * near, cells))
-        placed = (dot(h, sel_t[m]) + dot(l, sel_t[m])).reshape(nz, near, full)
-        cw[m] = placed
-
-    t1 = dot(r3[...], wy3[...])
-    for k in range(PATCH):
-        h, l = split(t1[k * wide : (k + 1) * wide])
-        h, l = split(dot(g3, jnp.concatenate([h, l, h], axis=0)) * dinv[k])
-        back = dot(b3, jnp.concatenate([h, l, h], axis=0))
-        put3(tb3, pl.ds(k * wide, wide), 0, qy, back)
-    fast = dot(tb3[...], wyt3[...]).reshape(PATCH, wide, full)
+            c = c + vz[:, k : k + 1] * dot_nt(zmodes[m], inv[m, k])[k : k + 1, :]
+        corr[m] = jnp.where(cut[m] >= 0, c, 0.0)
+
+    def cut_place(m):
+        h, l = split(jnp.where(spot[None], corr[m][:, None, :], 0.0).reshape(nz * near, cells))
+        cw[m] = (dot(h, sel_t[m]) + dot(l, sel_t[m])).reshape(nz, near, full)
+
+    def per_slot(step):
+        for m in range(slots):
+            step(m)
+
+    to_modes(0)
+    to_y(0)
+    for z in range(nz):
+        rs[z, :, pl.ds(0, ry)] = r0[z]
+        rs[z, :, pl.ds(ry, LANES)] = jnp.where(group_w == z, r1, 0.0)
+    to_modes(1)
+    per_slot(cut_take)
+    to_y(1)
+    solve_x(0)
+    to_modes(2)
+    to_y(2)
+    solve_x(1)
+    from_y(0)
+    to_modes(3)
+    per_slot(cut_solve)
+    to_y(3)
+    solve_x(2)
+    from_y(1)
+    per_slot(cut_place)
+    solve_x(3)
+    from_y(2)
+    from_y(3)
+
+    def fast_rows(k):
+        return fast[k // per][(k % per) * wide : (k % per + 1) * wide]
 
     def cut_part(z, start, count, lanes):
         tiles = []
@@ -434,14 +490,14 @@
     def total_rows(z, start, count):
         t = cut_part(z, start, count, pl.ds(0, ry))
         for k in range(PATCH):
-            t = t + basis_s[0, QUARTER + z, k] * fast[k, start : start + count, :ry]
+            t = t + basis_s[0, QUARTER + z, k] * fast_rows(k)[start : start + count, :ry]
         tot[z, pl.ds(start, count), :] = t
 
     packed = jnp.zeros((wide, LANES), f32)
     for z in range(nz):
         packed = jnp.where(group_w == z, cut_part(z, 0, wide, pl.ds(ry, LANES)), packed)
     for k in range(PATCH):
-        packed = packed + v_vec[k] * fast[k, :, ry:]
+        packed = packed + v_vec[k] * fast_rows(k)[:, ry:]
     edge[...] = packed
     for z in range(nz):
         total_rows(z, 0, HALO)

time: 18.1 us -> 17.2 us (0.950)
  Pallas kernels: 17.3 us -> 16.4 us
    pallas_call x1, Pallas kernels: 17.3 us -> 16.4 us  [on_device(): pl.pallas_call(functools.partial(kernel, sizes), out_shape=pltpu.VMEM(sta...]
where the time goes in v6:
time: 17.2 us; the launch traced here: 17.1 us
  Pallas kernels  16.4 us (95%)
  local copies, waits for them, and re-layouts  0.66 us (4%)
    pallas_call x1, Pallas kernels, on_device(): pl.pallas_call(functools.partial(kernel, sizes), out_shape=pltpu.VMEM(sta...  16.4 us
    unnamed x1, local copies, waits for them, and re-layouts  0.66 us

profile of v6, /device:TPU:13, one launch (start us, length us, event | category | flops | bytes accessed | tf_op | source)
XLA Modules:
  0.0 17.1 jit_solution(14010782563229185979)
XLA Ops:
  0.0 16.4 %shard_map.91 = f32[8,32,128]{2,1,0:T(8,128)S(1)} custom-call(f32[8,32,128]{2,1,0:T(8,128)} %state_h.1, bf16[8,32,128]{2,1,0:T(8,128)(2,1)} %load_h.1, s32[32,128]{1,0:T(8,128)} %active_h.1, f32[3,5]{1,0:T(4,128)} %stiff_h.1, f32[3,5]{1,0:T(4,128)} %mass_h.1, f32[3,16,16]{2,1,0:T(8,128)} %basis_h.1, f32[3,16]{1,0:T(4,128)} %values_h.1, s32[1,1,2]{2,1,0:T(1,128)} %cols_h.1, ...), custom_call_target="tpu_custom_call" | custom-call | tf_op jit(solution)/shard_map/pallas_call | solution.py:549
  16.4 0.7 %copy.11 = f32[8,32,128]{2,1,0:T(8,128)} copy(f32[8,32,128]{2,1,0:T(8,128)S(1)} %shard_map.91) | data formatting | bytes 262144

commit v7 on v6

--- a/solution.py
+++ b/solution.py
@@ -104,7 +104,7 @@
             (values_h, values), (cols_h, cols), (inverse_h, inv),
         ))
     ]
-    for fetch in fetches:
+    for fetch in fetches[:3]:
         fetch.start()
 
     own = pl.ds(HALO, rx)
@@ -125,6 +125,8 @@
         def _(d=d):
             pl.semaphore_signal(barrier, inc=1, device_id=device(*d), device_id_type=MESH)
 
+    for fetch in fetches[3:]:
+        fetch.start()
     for fetch in fetches[:3]:
         fetch.wait()
     for z in range(nz):
@@ -361,7 +363,7 @@
             lf[z, pl.ds(r, HALO), :] = pltpu.roll(tile, QUARTER, 0) if z % 2 else tile
     r0 = []
     r1 = jnp.zeros((wide, LANES), f32)
-    part_z = nz // 2
+    part_z = nz // 4
 
     def spread_y(g):
         for z in range(g * part_z, (g + 1) * part_z):
@@ -386,12 +388,16 @@
             r1 = jnp.where(group_w == z, applied[:, ry:], r1)
         return r1
 
+    parts = nz // part_z
+    bands = []
     spread_y(0)
-    first_half = band_y(0)
-    spread_y(1)
-    second_half = band_y(1)
-    r1 = band_x(0, *first_half, r1)
-    r1 = band_x(1, *second_half, r1)
+    for g in range(parts):
+        bands.append(band_y(g))
+        if g + 1 < parts:
+            spread_y(g + 1)
+        if g:
+            r1 = band_x(g - 1, *bands[g - 1], r1)
+    r1 = band_x(parts - 1, *bands[-1], r1)
     r1 = act_t * (load_t - r1)
 
     per = PATCH // 4
@@ -449,6 +455,21 @@
     def per_slot(step):
         for m in range(slots):
             step(m)
+
+    def fast_rows(k):
+        return fast[k // per][(k % per) * wide : (k % per + 1) * wide]
+
+    sums = {"edge": jnp.zeros((wide, LANES), f32)}
+    rims = [(z, start) for z in range(nz) for start in (0, HALO + rx)]
+    for key in rims:
+        sums[key] = jnp.zeros((HALO, ry), f32)
+
+    def add_group(g):
+        for k in range(g * per, (g + 1) * per):
+            rows = fast_rows(k)
+            sums["edge"] = sums["edge"] + v_vec[k] * rows[:, ry:]
+            for z, start in rims:
+                sums[z, start] = sums[z, start] + basis_s[0, QUARTER + z, k] * rows[start : start + HALO, :ry]
 
     to_modes(0)
     to_y(0)
@@ -470,11 +491,12 @@
     from_y(1)
     per_slot(cut_place)
     solve_x(3)
+    add_group(0)
     from_y(2)
+    add_group(1)
     from_y(3)
-
-    def fast_rows(k):
-        return fast[k // per][(k % per) * wide : (k % per + 1) * wide]
+    add_group(2)
+    add_group(3)
 
     def cut_part(z, start, count, lanes):
         tiles = []
@@ -496,12 +518,9 @@
     packed = jnp.zeros((wide, LANES), f32)
     for z in range(nz):
         packed = jnp.where(group_w == z, cut_part(z, 0, wide, pl.ds(ry, LANES)), packed)
-    for k in range(PATCH):
-        packed = packed + v_vec[k] * fast_rows(k)[:, ry:]
-    edge[...] = packed
-    for z in range(nz):
-        total_rows(z, 0, HALO)
-        total_rows(z, HALO + rx, HALO)
+    edge[...] = packed + sums["edge"]
+    for z, start in rims:
+        tot[z, pl.ds(start, HALO), :] = sums[z, start] + cut_part(z, start, HALO, pl.ds(0, ry))
     for j in range(nz // 2):
         for i, r, natural in ((0, HALO + rx, top), (1, 0, ~top)):
             odd = pltpu.roll(tot[2 * j + 1, pl.ds(r, HALO), :], QUARTER, 0)

time: 17.2 us -> 17.3 us (level)
  no operation moved by 1% of the time
where the time goes in v7:
time: 17.3 us; the launch traced here: 17.1 us
  Pallas kernels  16.4 us (95%)
  local copies, waits for them, and re-layouts  0.66 us (4%)
    pallas_call x1, Pallas kernels, on_device(): pl.pallas_call(functools.partial(kernel, sizes), out_shape=pltpu.VMEM(sta...  16.4 us
    unnamed x1, local copies, waits for them, and re-layouts  0.66 us

profile of v7, /device:TPU:13, one launch (start us, length us, event | category | flops | bytes accessed | tf_op | source)
XLA Modules:
  0.0 17.1 jit_solution(14030156050068804595)
XLA Ops:
  0.0 16.4 %shard_map.91 = f32[8,32,128]{2,1,0:T(8,128)S(1)} custom-call(f32[8,32,128]{2,1,0:T(8,128)} %state_h.1, bf16[8,32,128]{2,1,0:T(8,128)(2,1)} %load_h.1, s32[32,128]{1,0:T(8,128)} %active_h.1, f32[3,5]{1,0:T(4,128)} %stiff_h.1, f32[3,5]{1,0:T(4,128)} %mass_h.1, f32[3,16,16]{2,1,0:T(8,128)} %basis_h.1, f32[3,16]{1,0:T(4,128)} %values_h.1, s32[1,1,2]{2,1,0:T(1,128)} %cols_h.1, ...), custom_call_target="tpu_custom_call" | custom-call | tf_op jit(solution)/shard_map/pallas_call | solution.py:568
  16.4 0.7 %copy.11 = f32[8,32,128]{2,1,0:T(8,128)} copy(f32[8,32,128]{2,1,0:T(8,128)S(1)} %shard_map.91) | data formatting | bytes 262144

commit v8 on v7

--- a/solution.py
+++ b/solution.py
@@ -49,11 +49,6 @@
     u = (c - ry) & (HALF - 1)
     halo = jnp.where(u < QUARTER, u - QUARTER, ry + u - QUARTER)
     return jnp.where(c < ry, c, jnp.where(c < ry + LANES // 2, -1000, halo))
-
-
-def outer_y(r, ry):
-    u = (r - ry) & (HALF - 1)
-    return jnp.where(r < ry, r, jnp.where(r < ry + LANES // 2, u - HALO, ry + u))
 
 
 def wrap(v, n, reps):
@@ -218,25 +213,47 @@
 
     for fetch in fetches[3:9]:
         fetch.wait()
-    distance = jnp.abs(outer_y(iota((full, 1), 0), ry) - inner_y(iota((1, full), 1), ry))
+    pairs = groups // 2
+    short = iota((ry + 2 * PATCH, 1), 0)
+    spare = short & (HALF - 1)
+    reach = jnp.where(short < ry, short, jnp.where(short < ry + PATCH, spare - HALO, ry + spare))
+    distance = jnp.abs(reach - inner_y(iota((1, full), 1), ry))
     for j, taps in enumerate((mass, stiff)):
         h, l = split(band_of(distance, [taps[2, k] for k in range(BAND + 1)]))
+        cols_j = pl.ds(j * full, full)
         for i, part in enumerate((h, h, l)):
-            yb[pl.ds(i * full, full), pl.ds(j * full, full)] = part
+            yb[pl.ds(i * full, ry), cols_j] = part[:ry]
+            for side in range(2):
+                tile = part[ry + side * PATCH : ry + (side + 1) * PATCH]
+                for g in range(pairs):
+                    yb[pl.ds(i * full + ry + side * half + g * PATCH, PATCH), cols_j] = tile
 
     highest = lax.Precision.HIGHEST
     tile_y = jnp.dot(
         basis[2], (iota((PATCH, qy), 0) == (iota((PATCH, qy), 1) & (PATCH - 1))).astype(f32),
         precision=highest, preferred_element_type=f32,
     )
-    place = inner_y(iota((full, 1), 0), ry) + QUARTER - HALF * (iota((1, qy), 1) >> 4)
-    wy = jnp.zeros((full, qy), f32)
-    for t in range(PATCH):
-        wy = jnp.where(place == t, tile_y[t : t + 1, :], wy)
+    lane_b = iota((1, qy), 1) >> 4
+
+    def wy_tile(y):
+        place = y + QUARTER - HALF * lane_b
+        w = jnp.zeros((HALF, qy), f32)
+        for t in range(PATCH):
+            w = jnp.where(place == t, tile_y[t : t + 1, :], w)
+        return w
+
+    row8 = iota((HALF, 1), 0)
+    base = wy_tile(row8 + HALF)
+    tiles = []
+    for g in range(blocks_y):
+        shift = (PATCH * (g - 1)) % qy
+        moved = pltpu.roll(base, shift, 1) if shift else base
+        tiles.append(jnp.where(jnp.abs(lane_b - g) <= 1, moved, 0.0))
+    halo_tile = wy_tile(jnp.where(row8 < QUARTER, row8 - QUARTER, ry + row8 - QUARTER))
+    wy = jnp.concatenate(tiles + [jnp.zeros((half, qy), f32)] + [halo_tile] * groups, axis=0)
     h, l = split(wy)
     for i, part in enumerate((h, h, l)):
         wy3[pl.ds(i * full, full), :] = part
-
     h, l = split(wy.T)
     for i, part in enumerate((h, h, l)):
         wyt3[pl.ds(i * qy, qy), :] = part
@@ -260,7 +277,9 @@
 
     pad_r = -(-3 * wide // LANES) * LANES
     pad_c = -(-qx // LANES) * LANES
-    g3 = split3(wx_of((pad_r, pad_c), 3, 1).T[:qx, : 3 * wide], wide)
+    wx = wx_of((wide, pad_c), 1, 1)
+    wx = jnp.concatenate([wx] * 3 + [jnp.zeros((pad_r - 3 * wide, pad_c), f32)], axis=0)
+    g3 = split3(wx.T[:qx, : 3 * wide], wide)
     b3 = split3(wx_of((wide, 3 * qx), 1, 3), qx)
 
     c = iota((1, 4 * wide), 1)
@@ -301,13 +320,13 @@
             v = jnp.where(index == k, values[row, k], v)
         return v
 
-    lam = pick((qx, 1), 0, 1) + pick((1, qy), 1, 2)
+    lam = pick((PATCH, 1), 0, 1) + pick((1, qy), 1, 2)
     column = (iota((qx, 1), 0) >> 4) * blocks_y + (iota((1, qy), 1) >> 4)
     keep = jnp.ones((qx, qy), f32)
     for m in range(slots):
         keep = jnp.where(column == cut[m], 0.0, keep)
     for k in range(PATCH):
-        dinv[k] = keep / (values[0, k] + lam)
+        dinv[k] = keep * jnp.concatenate([1.0 / (values[0, k] + lam)] * blocks_x, axis=0)
 
     lane1 = iota((1, LANES), 1)
     group1 = (lane1 & (half - 1)) >> 3

time: 17.3 us -> 17.3 us (level)
  no operation moved by 1% of the time
where the time goes in v8:
time: 17.3 us; the launch traced here: 17.1 us
  Pallas kernels  16.4 us (95%)
  local copies, waits for them, and re-layouts  0.66 us (4%)
    pallas_call x1, Pallas kernels, on_device(): pl.pallas_call(functools.partial(kernel, sizes), out_shape=pltpu.VMEM(sta...  16.4 us
    unnamed x1, local copies, waits for them, and re-layouts  0.66 us

profile of v8, /device:TPU:13, one launch (start us, length us, event | category | flops | bytes accessed | tf_op | source)
XLA Modules:
  0.0 17.1 jit_solution(12226374333756194848)
XLA Ops:
  0.0 16.4 %shard_map.91 = f32[8,32,128]{2,1,0:T(8,128)S(1)} custom-call(f32[8,32,128]{2,1,0:T(8,128)} %state_h.1, bf16[8,32,128]{2,1,0:T(8,128)(2,1)} %load_h.1, s32[32,128]{1,0:T(8,128)} %active_h.1, f32[3,5]{1,0:T(4,128)} %stiff_h.1, f32[3,5]{1,0:T(4,128)} %mass_h.1, f32[3,16,16]{2,1,0:T(8,128)} %basis_h.1, f32[3,16]{1,0:T(4,128)} %values_h.1, s32[1,1,2]{2,1,0:T(1,128)} %cols_h.1, ...), custom_call_target="tpu_custom_call" | custom-call | tf_op jit(solution)/shard_map/pallas_call | solution.py:587
  16.4 0.7 %copy.11 = f32[8,32,128]{2,1,0:T(8,128)} copy(f32[8,32,128]{2,1,0:T(8,128)S(1)} %shard_map.91) | data formatting | bytes 262144

commit v9 on v8

--- a/solution.py
+++ b/solution.py
@@ -134,28 +134,6 @@
             odd = pltpu.roll(lf[2 * j + 1, pl.ds(r, HALO), :], QUARTER, 0)
             ext[nz + 1 + j, pl.ds(r, HALO), :] = jnp.where(natural, lf[2 * j, pl.ds(r, HALO), :], odd)
 
-    lane = iota((rx, LANES), 1)
-    group = (lane & (half - 1)) >> 3
-    high = lane >= half
-    lows = (lane & (HALF - 1)) < QUARTER
-    to_right = jnp.zeros((rx, LANES), f32)
-    to_left = jnp.zeros((rx, LANES), f32)
-    act = ext[nz, own, :]
-    for z in range(nz):
-        s = ext[z, own, :]
-        l = pltpu.roll(lf[z, own, :], (half + QUARTER + HALF * z) % LANES, 1)
-        mine = group == z
-        first = mine & high & lows
-        second = mine & high & ~lows
-        to_right = jnp.where(mine & ~high, pltpu.roll(s, (HALF + HALF * z) % LANES, 1), to_right)
-        to_right = jnp.where(first, l, to_right)
-        to_right = jnp.where(second, pltpu.roll(act, (half + HALF + HALF * z) % LANES, 1), to_right)
-        to_left = jnp.where(mine & ~high, pltpu.roll(s, HALF * z, 1) if z else s, to_left)
-        to_left = jnp.where(second, l, to_left)
-        to_left = jnp.where(first, pltpu.roll(act, (half + HALF * z) % LANES, 1), to_left)
-    pack_right[...] = to_right
-    pack_left[...] = to_left
-
     def copy1(i):
         dx, dy = DIRS[i]
         if dy == 0:
@@ -190,8 +168,8 @@
             device_id=device(dx, dy), device_id_type=MESH,
         )
 
-    def start_all(copy):
-        for i, d in enumerate(DIRS):
+    def start_all(copy, first=0, last=len(DIRS)):
+        for i, d in enumerate(DIRS[first:last], first):
             @pl.when(exists(*d))
             def _(i=i):
                 copy(i).start()
@@ -209,7 +187,30 @@
                 copy(i).wait_send()
 
     pl.semaphore_wait(barrier, count)
-    start_all(copy1)
+    start_all(copy1, last=2)
+
+    lane = iota((rx, LANES), 1)
+    group = (lane & (half - 1)) >> 3
+    high = lane >= half
+    lows = (lane & (HALF - 1)) < QUARTER
+    to_right = jnp.zeros((rx, LANES), f32)
+    to_left = jnp.zeros((rx, LANES), f32)
+    act = ext[nz, own, :]
+    for z in range(nz):
+        s = ext[z, own, :]
+        l = pltpu.roll(lf[z, own, :], (half + QUARTER + HALF * z) % LANES, 1)
+        mine = group == z
+        first = mine & high & lows
+        second = mine & high & ~lows
+        to_right = jnp.where(mine & ~high, pltpu.roll(s, (HALF + HALF * z) % LANES, 1), to_right)
+        to_right = jnp.where(first, l, to_right)
+        to_right = jnp.where(second, pltpu.roll(act, (half + HALF + HALF * z) % LANES, 1), to_right)
+        to_left = jnp.where(mine & ~high, pltpu.roll(s, HALF * z, 1) if z else s, to_left)
+        to_left = jnp.where(second, l, to_left)
+        to_left = jnp.where(first, pltpu.roll(act, (half + HALF * z) % LANES, 1), to_left)
+    pack_right[...] = to_right
+    pack_left[...] = to_left
+    start_all(copy1, first=2)
 
     for fetch in fetches[3:9]:
         fetch.wait()

time: 17.3 us -> 17.3 us (level)
  no operation moved by 1% of the time
where the time goes in v9:
time: 17.3 us; the launch traced here: 17.1 us
  Pallas kernels  16.4 us (95%)
  local copies, waits for them, and re-layouts  0.66 us (4%)
    pallas_call x1, Pallas kernels, on_device(): pl.pallas_call(functools.partial(kernel, sizes), out_shape=pltpu.VMEM(sta...  16.4 us
    unnamed x1, local copies, waits for them, and re-layouts  0.66 us

profile of v9, /device:TPU:13, one launch (start us, length us, event | category | flops | bytes accessed | tf_op | source)
XLA Modules:
  0.0 17.1 jit_solution(1126090410623444816)
XLA Ops:
  0.0 16.4 %shard_map.91 = f32[8,32,128]{2,1,0:T(8,128)S(1)} custom-call(f32[8,32,128]{2,1,0:T(8,128)} %state_h.1, bf16[8,32,128]{2,1,0:T(8,128)(2,1)} %load_h.1, s32[32,128]{1,0:T(8,128)} %active_h.1, f32[3,5]{1,0:T(4,128)} %stiff_h.1, f32[3,5]{1,0:T(4,128)} %mass_h.1, f32[3,16,16]{2,1,0:T(8,128)} %basis_h.1, f32[3,16]{1,0:T(4,128)} %values_h.1, s32[1,1,2]{2,1,0:T(1,128)} %cols_h.1, ...), custom_call_target="tpu_custom_call" | custom-call | tf_op jit(solution)/shard_map/pallas_call | solution.py:588
  16.4 0.7 %copy.11 = f32[8,32,128]{2,1,0:T(8,128)} copy(f32[8,32,128]{2,1,0:T(8,128)S(1)} %shard_map.91) | data formatting | bytes 262144
